TPU v7x, 32 devices: a whole 2x2x4 slice. The times are simulated.
32 devices in a mesh: grp: 2 (over y), term: 4 (over z), sec: 2 (over x), sub: 2 (over core).
Axes of the slice: x: 2, y: 2, z: 4, core: 2. Of those that a mesh axis runs over, the one named last changes fastest.
Arguments:
- wavefunction: float32 [8, 8, 256, 256], P(('grp', 'sec'), None, None, 'sub'), parts along dimension 0, may hold values from -6 to 6
- left_operators: float32 [12, 8, 256, 256], P('term', ('grp', 'sec')), parts along dimension 1, may hold values from -0.5 to 0.5
- right_operators: float32 [12, 8, 256, 256], P('term', ('grp', 'sec'), 'sub'), parts along dimension 1, may hold values from -0.109375 to 0.109375
- source_sectors: int32 [12, 8], P('term', ('grp', 'sec')), parts along dimension 1, may hold values from 0 to 3, as said below
Outputs:
- sigma_blocks: float32 [8, 8, 256, 256], P(('grp', 'sec'), None, 'term', 'sub'), parts along dimension 0
There are 2 independent parts, one for each index of `grp`. A program takes and returns all parts, laid end to end along the dimension named above; each array names one. Nothing has to cross between parts.
Inputs may be any that keep to these rules, and one draw needn't show every extreme that they name: source_sectors[t, s] differs from s by at most 1.
All inputs are finite; a program needn't handle non-finite values.
Results may differ from a plain program's by a relative error of at most 0.0003.
Values sent between devices are 32-bit elements; how exact they have to be, the bound alone decides.
No kernel may reach another device: no remote copies, remote signals or barrier semaphores. Data moves between devices by JAX's collectives and lax.ppermute only.
A program may use at most 64 MiB of HBM per device.

v0:
```python
import jax
import jax.numpy as jnp
from jax import lax
from jax.sharding import PartitionSpec as P

REACH = 1


def extended(value, sides, width):
    for axis, dim in sides:
        peers, length = (lax.axis_size(axis), value.shape[dim])
        up = [(i, (i + 1) % peers) for i in range(peers - 1)]
        down = [(j, i) for i, j in up]
        last = lax.slice_in_dim(value, length - width, length, axis=dim)
        initial = lax.slice_in_dim(value, 0, width, axis=dim)
        before = lax.ppermute(last, axis, up)
        after = lax.ppermute(initial, axis, down)
        value = jnp.concatenate([before, value, after], axis=dim)
    return value


def shards(wavefunction, left_operators, right_operators, source_sectors):
    highest = lax.Precision.HIGHEST
    sectors = wavefunction.shape[0]
    padded = extended(wavefunction, (("sec", 0),), REACH)
    lowest = lax.axis_index("sec") * sectors - REACH
    relative = source_sectors - lowest
    picked = jnp.take(padded, relative, axis=0)
    middle = jnp.einsum("tsvjk,tskl->tsvjl", picked, right_operators, precision=highest)
    partial_sum = jnp.einsum("tsij,tsvjl->svil", left_operators, middle, precision=highest)
    reduced = lax.psum_scatter(partial_sum, "term", scatter_dimension=2, tiled=True)
    return lax.psum_scatter(reduced, "sub", scatter_dimension=3, tiled=True)


def solution(mesh):
    in_specs = (
        P(("grp", "sec"), None, None, "sub"),
        P("term", ("grp", "sec"), None, None),
        P("term", ("grp", "sec"), "sub", None),
        P("term", ("grp", "sec")),
    )
    out_specs = P(("grp", "sec"), None, "term", "sub")
    return jax.shard_map(shards, mesh=mesh, in_specs=in_specs, out_specs=out_specs, check_vma=False)
```

profile of v0, /device:TPU:0, one launch (start us, length us, event | category | flops | bytes accessed | tf_op | source)
XLA Modules:
  0.0 180.2 jit_solution(8234396809647336103)
XLA Ops:
  6.5 0.0 copy-start
  6.5 0.0 copy-start.2
  6.5 0.0 reduce-scatter.3.cloned.1.call-start
  6.5 2.8 %fusion.6 = (f32[1,8,256,128]{3,2,1,0:T(8,128)}, f32[1,8,256,128]{3,2,1,0:T(8,128)S(1)}) fusion(f32[2,8,256,128]{3,2,1,0:T(8,128)} %param.4), kind=kLoop, calls=%fused_computation.13 | loop fusion | bytes 4194304 | tf_op jit(solution)/shard_map/slice | solution.py:14
  9.4 5.9 %collective-permute-start = (f32[1,8,256,128]{3,2,1,0:T(8,128)}, f32[1,8,256,128]{3,2,1,0:T(8,128)}, u32[]{:S(2)}, u32[]{:S(2)}) collective-permute-start(f32[1,8,256,128]{3,2,1,0:T(8,128)} %get-tuple-element.7), channel_id=1, source_target_pairs={{0,2},{1,3},{4,6},{5,7},{8,10},{9,11},{12,14},{13,15},{16,18},{17,... | collective-permute-start | bytes 3145736 | tf_op jit(solution)/shard_map/ppermute | solution.py:16
  15.3 1.3 collective-permute-start.1
  16.5 0.0 copy-done.2
  16.6 0.1 copy.13
  16.7 0.1 reshape.7
  16.8 20.2 %collective-permute-done = f32[1,8,256,128]{3,2,1,0:T(8,128)} collective-permute-done((f32[1,8,256,128]{3,2,1,0:T(8,128)}, f32[1,8,256,128]{3,2,1,0:T(8,128)}, u32[]{:S(2)}, u32[]{:S(2)}) %collective-permute-start) | collective-permute-done | bytes 1048608 | tf_op jit(solution)/shard_map/ppermute | solution.py:16
  36.9 4.9 %collective-permute-done.1 = f32[1,8,256,128]{3,2,1,0:T(8,128)} collective-permute-done((f32[1,8,256,128]{3,2,1,0:T(8,128)S(1)}, f32[1,8,256,128]{3,2,1,0:T(8,128)}, u32[]{:S(2)}, u32[]{:S(2)}) %collective-permute-start.1) | collective-permute-done | bytes 1048608 | tf_op jit(solution)/shard_map/ppermute | solution.py:17
  41.9 4.6 %pad_maximum_fusion = f32[4,8,256,128]{3,2,1,0:T(8,128)} fusion(f32[1,8,256,128]{3,2,1,0:T(8,128)} %collective-permute-done.1, f32[2,8,256,128]{3,2,1,0:T(8,128)} %param.4, f32[1,8,256,128]{3,2,1,0:T(8,128)} %collective-permute-done), kind=kLoop, calls=%fused_computation.3 | loop fusion | flops 2097152 | bytes 8388608 | tf_op jit(solution)/shard_map/concatenate | solution.py:18
  46.5 0.0 copy-start.1
  46.5 5.9 %gather_fusion = f32[6,8,256,128]{3,2,1,0:T(8,128)} fusion(f32[4,8,256,128]{3,2,1,0:T(8,128)} %pad_maximum_fusion, s32[1024]{0:T(1024)S(1)} %pad_clamp_fusion), kind=kCustom, calls=%fused_computation | custom fusion | bytes 12582936 | tf_op jit(solution)/shard_map/jit(_take)/gather | solution.py:28
  52.4 0.0 copy-done.1
  52.4 12.9 %fusion = f32[3,2,8,256,256]{3,4,0,2,1:T(8,128)S(1)} fusion(f32[3,2,8,256,128]{4,3,2,1,0:T(8,128)} %bitcast.15, pred[3,2]{0,1:T(4,128)(4,1)S(1)} %get-tuple-element.5, f32[3,2,128,256]{3,2,1,0:T(8,128)S(1)} %copy-done.1), kind=kOutput, calls=%fused_computation.2 | convolution fusion | flops 4833411072 | bytes 19660806 | tf_op jit(solution)/shard_map/tsvjk,tskl->tsvjl/dot_general | solution.py:29
  65.2 0.0 copy-done
  65.3 11.9 %convolution_bitcast_fusion = f32[2,8,256,256]{2,3,1,0:T(8,128)} fusion(f32[3,2,8,256,256]{3,4,0,2,1:T(8,128)S(1)} %fusion, f32[3,2,256,256]{3,2,1,0:T(8,128)S(1)} %copy-done), kind=kOutput, calls=%fused_computation.6 | convolution fusion | flops 9663676416 | bytes 18350080 | tf_op jit(solution)/shard_map/tsij,tsvjl->svil/dot_general | solution.py:30
  77.2 5.5 %copy.18 = f32[2,8,256,256]{3,1,0,2:T(8,128)} copy(f32[2,8,256,256]{2,3,1,0:T(8,128)} %convolution_bitcast_fusion) | data formatting | bytes 8388608 | tf_op jit(solution)/shard_map/tsij,tsvjl->svil/transpose | solution.py:30
  82.6 0.0 reduce-scatter.3.cloned.1.call-update
  82.7 0.0 reduce-scatter.5.cloned.1.call-start
  82.7 77.2 %reduce-scatter.3.cloned.1.call-done = f32[2,8,64,256]{3,1,0,2:T(8,128)} async-done(((f32[2,8,256,256]{3,1,0,2:T(8,128)}), f32[2,8,64,256]{3,1,0,2:T(8,128)}) %reduce-scatter.3.cloned.1.call-update) | async-done | bytes 1048592 | tf_op jit(solution)/shard_map/reduce_scatter | solution.py:31
  159.9 0.0 reduce-scatter.5.cloned.1.call-update
  159.9 11.4 %reduce-scatter.5.cloned.1.call-done = f32[2,8,64,128]{3,1,0,2:T(8,128)} async-done(((f32[2,8,64,256]{3,1,0,2:T(8,128)}), f32[2,8,64,128]{3,1,0,2:T(8,128)}) %reduce-scatter.5.cloned.1.call-update) | async-done | bytes 524304 | tf_op jit(solution)/shard_map/reduce_scatter | solution.py:32
  171.3 2.0 %copy.19 = f32[2,8,64,128]{3,2,1,0:T(8,128)} copy(f32[2,8,64,128]{3,1,0,2:T(8,128)} %reduce-scatter.5.cloned.1.call-done) | data formatting | bytes 1048576 | tf_op jit(solution)/shard_map/reduce_scatter | solution.py:32
  (2 shorter events, 0.0 us)
Async XLA Ops:
  6.5 58.7 %copy-start = (f32[3,2,256,256]{3,2,1,0:T(8,128)S(1)}, f32[3,2,256,256]{3,2,1,0:T(8,128)}, u32[]{:S(2)}) copy-start(f32[3,2,256,256]{3,2,1,0:T(8,128)} %param.5) | copy-start | bytes 4718596
  6.5 10.0 %copy-start.2 = (s32[3,2]{0,1:T(2,128)S(1)}, s32[3,2]{0,1:T(2,128)}, u32[]{:S(2)}) copy-start(s32[3,2]{0,1:T(2,128)} %param.7) | copy-start | bytes 76
  6.5 153.4 %reduce-scatter.3.cloned.1.call-start = ((), (), s32[]{:S(2)}) async-start(), calls=%async_computation.2 | async-start | bytes 5242880 | tf_op jit(solution)/shard_map/reduce_scatter | solution.py:31
  9.4 27.6 %collective-permute-start = (f32[1,8,256,128]{3,2,1,0:T(8,128)}, f32[1,8,256,128]{3,2,1,0:T(8,128)}, u32[]{:S(2)}, u32[]{:S(2)}) collective-permute-start(f32[1,8,256,128]{3,2,1,0:T(8,128)} %get-tuple-element.7), channel_id=1, source_target_pairs={{0,2},{1,3},{4,6},{5,7},{8,10},{9,11},{12,14},{13,15},{16,18},{17,... | collective-permute-start | bytes 3145736 | tf_op jit(solution)/shard_map/ppermute | solution.py:16
  15.3 26.6 %collective-permute-start.1 = (f32[1,8,256,128]{3,2,1,0:T(8,128)S(1)}, f32[1,8,256,128]{3,2,1,0:T(8,128)}, u32[]{:S(2)}, u32[]{:S(2)}) collective-permute-start(f32[1,8,256,128]{3,2,1,0:T(8,128)S(1)} %get-tuple-element.8), channel_id=1, source_target_pairs={{2,0},{3,1},{6,4},{7,5},{10,8},{11,9},{14,12},{15,13},{18,16},{19,... | collective-permute-start | bytes 3145736 | tf_op jit(solution)/shard_map/ppermute | solution.py:17
  46.5 5.9 %copy-start.1 = (f32[3,2,128,256]{3,2,1,0:T(8,128)S(1)}, f32[3,2,128,256]{3,2,1,0:T(8,128)}, u32[]{:S(2)}) copy-start(f32[3,2,128,256]{3,2,1,0:T(8,128)} %param.6) | copy-start | bytes 2359300
  82.7 88.7 %reduce-scatter.5.cloned.1.call-start = ((), (), s32[]{:S(2)}) async-start(), calls=%async_computation.3 | async-start | bytes 1572864 | tf_op jit(solution)/shard_map/reduce_scatter | solution.py:32
Sparse Core Ops, SparseCore 0:
  82.8 77.0 reduce-scatter.2
  162.2 9.0 reduce-scatter.4
where the time goes:
time: 180 us
  waiting for transfers between devices  114 us (63%)
  matrix products  24.8 us (14%)
  local copies, waits for them, and re-layouts  16.4 us (9%)
  between operations  13.4 us (7%)
  starting transfers between devices  7.19 us (4%)
  other arithmetic  4.66 us (3%)
    reduce_scatter x1, waiting for transfers between devices, shards(): lax.psum_scatter(partial_sum, 'term', scatter_dimension=2, tiled=True)  77.2 us
    ppermute x1, waiting for transfers between devices, extended(): before = lax.ppermute(last, axis, up)  20.2 us
    dot_general x1, matrix products, shards(): jnp.einsum('tsvjk,tskl->tsvjl', picked, right_operators, precision=highest)  12.9 us
    dot_general x1, matrix products, shards(): jnp.einsum('tsij,tsvjl->svil', left_operators, middle, precision=highest)  11.9 us
    reduce_scatter x1, waiting for transfers between devices, shards(): return lax.psum_scatter(reduced, 'sub', scatter_dimension=3, tiled=True)  11.4 us
    ppermute x1, starting transfers between devices, extended(): before = lax.ppermute(last, axis, up)  5.87 us
    gather x1, local copies, waits for them, and re-layouts, shards(): picked = jnp.take(padded, relative, axis=0)  5.87 us
    transpose x1, local copies, waits for them, and re-layouts, shards(): jnp.einsum('tsij,tsvjl->svil', left_operators, middle, precision=highest)  5.49 us
  transfers between devices with their start and end apart: 4, of which 4 were waited for; matrix products, arithmetic and copies ran while one was open for 0% of the time, Pallas kernels for 0%

commit v1 on v0

v1 whole, which is shorter than its diff:
```python
import functools

import jax
import jax.numpy as jnp
from jax import lax
from jax.experimental import pallas as pl
from jax.experimental.pallas import tpu as pltpu
from jax.sharding import PartitionSpec as P

CHUNKS = 2


def halving_order(peers):
    bits = peers.bit_length() - 1
    assert peers == 1 << bits
    return sorted(range(peers), key=lambda m: -sum(((m >> b) & 1) << (bits - 1 - b) for b in range(bits)))


def halves(value):
    high = value.astype(jnp.bfloat16)
    return high, (value - high.astype(jnp.float32)).astype(jnp.bfloat16)


def chunk_kernel(order, terms, with_halo, scalars, *refs):
    left, right_own, right_other, psi = refs[:4]
    halo = refs[4] if with_halo else None
    own, other, left_cat, right_cat, psi_cat, mid_cat = refs[4 + with_halo:]
    rows, depth = left.shape[2], left.shape[3]
    width = psi.shape[3]
    piece = rows // len(order)
    columns = right_own.shape[3]

    @pl.when(pl.program_id(0) == 0)
    def _():
        for t in range(terms):
            ordered = [left[t, 0, pl.ds(pl.multiple_of((scalars[1] ^ m) * piece, piece), piece), :] for m in order]
            high, low = halves(jnp.concatenate(ordered, axis=0))
            left_cat[t, :, 0:depth] = high
            left_cat[t, :, depth:2 * depth] = high
            left_cat[t, :, 2 * depth:3 * depth] = low
            for at, ref in ((0, right_own), (columns, right_other)):
                high, low = halves(ref[t, 0])
                start = t * 3 * width
                right_cat[start:start + width, at:at + columns] = high
                right_cat[start + width:start + 2 * width, at:at + columns] = high
                right_cat[start + 2 * width:start + 3 * width, at:at + columns] = low

    for source in range(2 + with_halo):
        for v in range(2):
            high, low = halves(psi[source, v] if source < 2 else halo[v])
            psi_cat[source, 0:depth, v * width:(v + 1) * width] = high
            psi_cat[source, depth:2 * depth, v * width:(v + 1) * width] = low
            psi_cat[source, 2 * depth:3 * depth, v * width:(v + 1) * width] = high
    for t in range(terms):
        mid = jnp.dot(left_cat[t], psi_cat[scalars[3 + t]], preferred_element_type=jnp.float32)
        high, low = halves(mid)
        for v in range(2):
            start = t * 3 * width
            mid_cat[v * rows:(v + 1) * rows, start:start + width] = high[:, v * width:(v + 1) * width]
            mid_cat[v * rows:(v + 1) * rows, start + width:start + 2 * width] = low[:, v * width:(v + 1) * width]
            mid_cat[v * rows:(v + 1) * rows, start + 2 * width:start + 3 * width] = high[:, v * width:(v + 1) * width]
    total = jnp.dot(mid_cat[...], right_cat[...], preferred_element_type=jnp.float32)
    for v in range(2):
        for p in range(len(order)):
            start = v * rows + p * piece
            own[p, v] = total[start:start + piece, 0:columns]
            other[p, v] = total[start:start + piece, columns:2 * columns]


def chunk(scalars, left, right, psi, halo, first, count, order):
    terms, _, rows, depth = left.shape
    width, columns = psi.shape[3], right.shape[3] // 2
    piece = rows // len(order)
    lead = first // 2
    with_halo = halo is not None
    in_specs = [
        pl.BlockSpec((terms, 1, rows, depth), lambda i, s: (0, s[0], 0, 0)),
        pl.BlockSpec((terms, 1, width, columns), lambda i, s: (0, s[0], 0, s[2])),
        pl.BlockSpec((terms, 1, width, columns), lambda i, s: (0, s[0], 0, 1 - s[2])),
        pl.BlockSpec((2, 2, depth, width), lambda i, s: (0, lead + i, 0, 0)),
    ]
    args = [left, right, right, psi]
    if with_halo:
        in_specs.append(pl.BlockSpec((2, depth, width), lambda i, s: (i, 0, 0)))
        args.append(halo)
    out = jax.ShapeDtypeStruct((len(order), count, piece, columns), jnp.float32)
    out_spec = pl.BlockSpec((len(order), 2, piece, columns), lambda i, s: (0, i, 0, 0))
    flops = 2 * 3 * terms * count * rows * width * (depth + 2 * columns)
    return pl.pallas_call(
        functools.partial(chunk_kernel, order, terms, with_halo),
        out_shape=(out, out),
        grid_spec=pltpu.PrefetchScalarGridSpec(
            num_scalar_prefetch=1,
            grid=(count // 2,),
            in_specs=in_specs,
            out_specs=(out_spec, out_spec),
            scratch_shapes=[
                pltpu.VMEM((terms, rows, 3 * depth), jnp.bfloat16),
                pltpu.VMEM((terms * 3 * width, 2 * columns), jnp.bfloat16),
                pltpu.VMEM((2 + with_halo, 3 * depth, 2 * width), jnp.bfloat16),
                pltpu.VMEM((2 * rows, terms * 3 * width), jnp.bfloat16),
            ],
        ),
        compiler_params=pltpu.CompilerParams(vmem_limit_bytes=32 * 1024 * 1024),
        cost_estimate=pl.CostEstimate(flops=flops, bytes_accessed=8 * 1024 * 1024, transcendentals=0),
        name="terms_of_sector",
    )(scalars, *args)


def shards(wavefunction, left_operators, right_operators, source_sectors):
    sectors, vectors = wavefunction.shape[:2]
    assert sectors == 2
    peers, places = lax.axis_size("term"), lax.axis_size("sec")
    z, x, core = lax.axis_index("term"), lax.axis_index("sec"), lax.axis_index("sub")
    order = halving_order(peers)
    stages = [[(i, i ^ (1 << b)) for i in range(peers)] for b in range(peers.bit_length() - 1)]
    swap = [(0, 1), (1, 0)]
    relative = source_sectors - x * sectors
    picks = jnp.where((relative >= 0) & (relative < sectors), relative, 2)
    count = vectors // CHUNKS

    targets = (x, 1 - x) if places == 2 else (jnp.int32(0), jnp.int32(1))

    def halo_of(which, first):
        if places == 2:
            if which == 0:
                return None
            edge, perm = targets[1], swap
        elif which == 0:
            edge, perm = jnp.int32(1), [(i, i + 1) for i in range(places - 1)]
        else:
            edge, perm = jnp.int32(0), [(i + 1, i) for i in range(places - 1)]
        sent = lax.dynamic_slice(wavefunction, (edge, first, 0, 0), (1, count) + wavefunction.shape[2:])[0]
        return lax.ppermute(sent, "sec", perm)

    work = [(which, first) for which in range(2) for first in range(0, vectors, count)]
    halos = {item: halo_of(*item) for item in work}
    done = {}
    for which, first in work:
        target = targets[which]
        scalars = jnp.concatenate([jnp.stack([target, z, core]), lax.dynamic_index_in_dim(picks, target, 1, keepdims=False)])
        own, other = chunk(scalars, left_operators, right_operators, wavefunction, halos[which, first], first, count, order)
        addends = [own, lax.ppermute(other, "sub", swap)]
        for perm in stages:
            half = addends[0].shape[0] // 2
            sent = sum(a[:half] for a in addends)
            addends = [a[half:] for a in addends] + [lax.ppermute(sent, "term", perm)]
        done[which, first] = sum(a[0] for a in addends)
    outs = [jnp.concatenate([done[which, first] for first in range(0, vectors, count)], axis=0) for which in range(2)]
    if places == 2:
        outs = [jnp.where(x == 0, outs[0], outs[1]), jnp.where(x == 0, outs[1], outs[0])]
    return jnp.stack(outs)


def solution(mesh):
    in_specs = (
        P(("grp", "sec"), None, None, "sub"),
        P("term", ("grp", "sec"), None, None),
        P("term", ("grp", "sec"), "sub", None),
        P("term", ("grp", "sec")),
    )
    out_specs = P(("grp", "sec"), None, "term", "sub")
    return jax.shard_map(shards, mesh=mesh, in_specs=in_specs, out_specs=out_specs, check_vma=False)
```

time: 180 us -> 76.7 us (0.43)
  waiting for transfers between devices: 114 us -> 30.8 us
  matrix products: 24.8 us -> 0 us
  Pallas kernels: 0 us -> 15.5 us
  between operations: 13.4 us -> 0.13 us
  local copies, waits for them, and re-layouts: 16.4 us -> 8.39 us
  starting transfers between devices: 7.19 us -> 14.5 us
  other arithmetic: 4.66 us -> 6.96 us
    reduce_scatter x2 -> x0, waiting for transfers between devices: 88.6 us -> none  [the longest x1 77.2 us: shards(): lax.psum_scatter(partial_sum, 'term', scatter_dimension=2, tiled=True)]
    dot_general x2 -> x0, matrix products: 24.8 us -> none  [the longest x1 12.9 us: shards(): jnp.einsum('tsvjk,tskl->tsvjl', picked, right_operators, precision=highest)]
    pallas_call x0 -> x4, Pallas kernels: none -> 15.5 us  [chunk(): pl.pallas_call(functools.partial(chunk_kernel, order, terms, with_halo),...]
    ppermute x2 -> x14, starting transfers between devices: 7.15 us -> 14.5 us  [the longest x8 10.9 us: shards(): addends = [a[half:] for a in addends] + [lax.ppermute(sent, 'term', perm)]]
    unnamed x6 -> x20, local copies, waits for them, and re-layouts: 0.01 us -> 6.04 us
    add x0 -> x12, other arithmetic: none -> 5.92 us  [the longest x8 3.97 us: shards(): sent = sum((a[:half] for a in addends))]
    gather x1 -> x0, local copies, waits for them, and re-layouts: 5.87 us -> none  [shards(): picked = jnp.take(padded, relative, axis=0)]
    ppermute x2 -> x14, waiting for transfers between devices: 25.1 us -> 30.8 us  [the longest x8 26 us: shards(): addends = [a[half:] for a in addends] + [lax.ppermute(sent, 'term', perm)]]
  transfers between devices with their start and end apart: 4 -> 14, of which waited for: 4 -> 5; matrix products, arithmetic and copies ran while one was open for 0% -> 8% of each run, Pallas kernels for 0% -> 20%
where the time goes in v1:
time: 76.7 us; the launch traced here: 76.3 us
  waiting for transfers between devices  30.8 us (40%)
  Pallas kernels  15.5 us (20%)
  starting transfers between devices  14.5 us (19%)
  local copies, waits for them, and re-layouts  8.39 us (11%)
  other arithmetic  6.96 us (9%)
    ppermute x8, waiting for transfers between devices, shards(): addends = [a[half:] for a in addends] + [lax.ppermute(sent, 'term', perm)]  26 us
    pallas_call x4, Pallas kernels, chunk(): pl.pallas_call(functools.partial(chunk_kernel, order, terms, with_halo),...  15.5 us
    ppermute x8, starting transfers between devices, shards(): addends = [a[half:] for a in addends] + [lax.ppermute(sent, 'term', perm)]  10.9 us
    unnamed x20, local copies, waits for them, and re-layouts  6.04 us
    ppermute x2, waiting for transfers between devices, halo_of(): return lax.ppermute(sent, 'sec', perm)  4.88 us
    add x8, other arithmetic, shards(): sent = sum((a[:half] for a in addends))  3.97 us
    ppermute x2, starting transfers between devices, halo_of(): return lax.ppermute(sent, 'sec', perm)  2.95 us
    squeeze x1, local copies, waits for them, and re-layouts, halo_of(): lax.dynamic_slice(wavefunction, (edge, first, 0, 0), (1, count) + wavefun...  2.35 us
  transfers between devices with their start and end apart: 14, of which 5 were waited for; matrix products, arithmetic and copies ran while one was open for 8% of the time, Pallas kernels for 20%

profile of v1, /device:TPU:0, one launch (start us, length us, event | category | flops | bytes accessed | tf_op | source)
XLA Modules:
  0.0 76.3 jit_solution(5134528591874164087)
XLA Ops:
  0.0 0.0 copy-start.9
  0.0 0.0 copy-start
  0.0 2.3 %dynamic-slice_bitcast_fusion.1 = (f32[4,256,128]{2,1,0:T(8,128)}, f32[4,256,128]{2,1,0:T(8,128)}) fusion(f32[2,8,256,128]{3,2,1,0:T(8,128)} %refs_3_.7, s32[]{:T(128)S(6)} %select_n.44), kind=kLoop, calls=%fused_computation.2 | loop fusion | bytes 2097156 | tf_op jit(solution)/shard_map/squeeze | solution.py:133
  2.4 2.9 %collective-permute-start.6 = (f32[4,256,128]{2,1,0:T(8,128)}, f32[4,256,128]{2,1,0:T(8,128)S(1)}, u32[]{:S(2)}, u32[]{:S(2)}) collective-permute-start(f32[4,256,128]{2,1,0:T(8,128)} %get-tuple-element.21), channel_id=1, source_target_pairs={{0,2},{2,0},{1,3},{3,1},{4,6},{6,4},{5,7},{7,5},{8,10},{10,8},{9,1... | collective-permute-start | bytes 1572872 | tf_op jit(solution)/shard_map/ppermute | solution.py:134
  5.3 0.0 copy-done.9
  5.3 0.1 pad_add_fusion.scalars
  5.4 0.0 copy-done
  5.4 0.0 copy-start.1
  5.4 1.6 %copy-done.1 = f32[2,8,256,128]{3,2,1,0:T(8,128)S(1)} copy-done((f32[2,8,256,128]{3,2,1,0:T(8,128)S(1)}, f32[2,8,256,128]{3,2,1,0:T(8,128)}, u32[]{:S(2)}) %copy-start.1) | copy-done | bytes 2097176
  7.0 0.0 copy-start.3
  7.0 1.4 %copy-done.3 = f32[3,2,256,256]{3,2,1,0:T(8,128)S(1)} copy-done((f32[3,2,256,256]{3,2,1,0:T(8,128)S(1)}, f32[3,2,256,256]{3,2,1,0:T(8,128)}, u32[]{:S(2)}) %copy-start.3) | copy-done | bytes 1572888
  8.4 4.0 %terms_of_sector.5 = (f32[4,4,64,128]{3,2,1,0:T(8,128)S(1)}, f32[4,4,64,128]{3,2,1,0:T(8,128)}) custom-call(s32[6]{0:T(128)S(1)} %pad_add_fusion.scalars, f32[3,2,256,256]{3,2,1,0:T(8,128)S(1)} %copy-done.3, f32[3,2,128,256]{3,2,1,0:T(8,128)S(1)} %copy-done, f32[3,2,128,256]{3,2,1,0:T(8,128)S(1)} %copy-done, f32[2,8,256,128]{3,2,1,0:T(8,128)S(1)} %copy-done.1), custom_call_target="tpu_custom_call" | custom-call | flops 1207959552 | bytes 8388608 | tf_op jit(solution)/shard_map/terms_of_sector/pallas_call | solution.py:89
  12.4 0.0 copy-start.7
  12.4 0.8 %copy-done.7 = f32[4,4,64,128]{3,2,1,0:T(8,128)} copy-done((f32[4,4,64,128]{3,2,1,0:T(8,128)}, f32[4,4,64,128]{3,2,1,0:T(8,128)S(1)}, u32[]{:S(2)}) %copy-start.7) | copy-done | bytes 524312
  13.2 0.0 copy-start.2
  13.2 0.0 collective-permute-start.3
  13.2 3.9 %terms_of_sector.4 = (f32[4,4,64,128]{3,2,1,0:T(8,128)S(1)}, f32[4,4,64,128]{3,2,1,0:T(8,128)}) custom-call(s32[6]{0:T(128)S(1)} %pad_add_fusion.scalars, f32[3,2,256,256]{3,2,1,0:T(8,128)S(1)} %copy-done.3, f32[3,2,128,256]{3,2,1,0:T(8,128)S(1)} %copy-done, f32[3,2,128,256]{3,2,1,0:T(8,128)S(1)} %copy-done, f32[2,8,256,128]{3,2,1,0:T(8,128)S(1)} %copy-done.1), custom_call_target="tpu_custom_call" | custom-call | flops 1207959552 | bytes 8388608 | tf_op jit(solution)/shard_map/terms_of_sector/pallas_call | solution.py:89
  17.1 0.0 copy-start.5
  17.1 0.8 %copy-done.5 = f32[4,4,64,128]{3,2,1,0:T(8,128)} copy-done((f32[4,4,64,128]{3,2,1,0:T(8,128)}, f32[4,4,64,128]{3,2,1,0:T(8,128)S(1)}, u32[]{:S(2)}) %copy-start.5) | copy-done | bytes 524312
  17.9 0.5 collective-permute-start
  18.4 0.0 collective-permute-start.10
  18.4 0.1 pad_add_fusion.1.scalars
  18.5 0.0 collective-permute-done.6.refs_4_
  18.5 0.0 copy-done.2
  18.5 0.0 copy-start.4
  18.5 1.4 %copy-done.4 = f32[3,2,256,256]{3,2,1,0:T(8,128)S(1)} copy-done((f32[3,2,256,256]{3,2,1,0:T(8,128)S(1)}, f32[3,2,256,256]{3,2,1,0:T(8,128)}, u32[]{:S(2)}) %copy-start.4) | copy-done | bytes 1572888
  19.9 0.0 copy-start.8
  19.9 0.0 copy-start.6
  19.9 3.4 %terms_of_sector.6 = (f32[4,4,64,128]{3,2,1,0:T(8,128)S(1)}, f32[4,4,64,128]{3,2,1,0:T(8,128)S(1)}) custom-call(s32[6]{0:T(128)S(1)} %pad_add_fusion.1.scalars, f32[3,2,256,256]{3,2,1,0:T(8,128)S(1)} %copy-done.4, f32[3,2,128,256]{3,2,1,0:T(8,128)S(1)} %copy-done, f32[3,2,128,256]{3,2,1,0:T(8,128)S(1)} %copy-done, f32[2,8,256,128]{3,2,1,0:T(8,128)S(1)} %copy-done.2, ...), custom_call_target="tpu_custom_call" | custom-call | flops 1207959552 | bytes 8388608 | tf_op jit(solution)/shard_map/terms_of_sector/pallas_call | solution.py:89
  23.3 0.1 collective-permute-start.7
  23.4 0.0 collective-permute-done.3
  23.4 0.0 copy-done.8
  23.4 1.0 %slice_add_fusion.2 = f32[2,4,64,128]{3,2,1,0:T(8,128)S(1)} fusion(f32[4,4,64,128]{3,2,1,0:T(8,128)} %collective-permute-done.3, f32[4,4,64,128]{3,2,1,0:T(8,128)S(1)} %copy-done.8), kind=kLoop, calls=%fused_computation.5 | loop fusion | flops 65536 | bytes 786432 | tf_op jit(solution)/shard_map/add | solution.py:146
  24.4 2.2 %collective-permute-start.4 = (f32[2,4,64,128]{3,2,1,0:T(8,128)S(1)}, f32[2,4,64,128]{3,2,1,0:T(8,128)S(1)}, u32[]{:S(2)}, u32[]{:S(2)}) collective-permute-start(f32[2,4,64,128]{3,2,1,0:T(8,128)S(1)} %slice_add_fusion.2), channel_id=1, source_target_pairs={{0,4},{4,0},{8,12},{12,8},{1,5},{5,1},{9,13},{13,9},{2,6},{6,2},{1... | collective-permute-start | bytes 786440 | tf_op jit(solution)/shard_map/ppermute | solution.py:147
  26.6 0.0 collective-permute-done
  26.6 0.0 copy-done.6
  26.6 1.0 %slice_add_fusion.3 = f32[2,4,64,128]{3,2,1,0:T(8,128)S(1)} fusion(f32[4,4,64,128]{3,2,1,0:T(8,128)} %collective-permute-done, f32[4,4,64,128]{3,2,1,0:T(8,128)S(1)} %copy-done.6), kind=kLoop, calls=%fused_computation.6 | loop fusion | flops 65536 | bytes 786432 | tf_op jit(solution)/shard_map/add | solution.py:146
  27.6 0.1 collective-permute-start.1
  27.7 4.9 %collective-permute-done.10.refs_4_ = f32[4,256,128]{2,1,0:T(8,128)} collective-permute-done((f32[4,256,128]{2,1,0:T(8,128)}, f32[4,256,128]{2,1,0:T(8,128)}, u32[]{:S(2)}, u32[]{:S(2)}) %collective-permute-start.10) | collective-permute-done | bytes 524320 | tf_op jit(solution)/shard_map/ppermute | solution.py:134
  32.6 4.2 %terms_of_sector.7 = (f32[4,4,64,128]{3,2,1,0:T(8,128)S(1)}, f32[4,4,64,128]{3,2,1,0:T(8,128)S(1)}) custom-call(s32[6]{0:T(128)S(1)} %pad_add_fusion.1.scalars, f32[3,2,256,256]{3,2,1,0:T(8,128)S(1)} %copy-done.4, f32[3,2,128,256]{3,2,1,0:T(8,128)S(1)} %copy-done, f32[3,2,128,256]{3,2,1,0:T(8,128)S(1)} %copy-done, f32[2,8,256,128]{3,2,1,0:T(8,128)S(1)} %copy-done.2, ...), custom_call_target="tpu_custom_call" | custom-call | flops 1207959552 | bytes 8388608 | tf_op jit(solution)/shard_map/terms_of_sector/pallas_call | solution.py:89
  36.8 0.1 collective-permute-start.11
  36.9 0.0 collective-permute-done.4
  36.9 0.9 %slice_add_fusion.12 = f32[1,4,64,128]{3,2,1,0:T(8,128)S(1)} fusion(f32[2,4,64,128]{3,2,1,0:T(8,128)S(1)} %collective-permute-done.4, f32[4,4,64,128]{3,2,1,0:T(8,128)} %collective-permute-done.3, f32[4,4,64,128]{3,2,1,0:T(8,128)S(1)} %copy-done.8), kind=kLoop, calls=%fused_computation.21 | loop fusion | flops 65536 | bytes 524288 | tf_op jit(solution)/shard_map/add | solution.py:146
  37.8 2.7 %collective-permute-start.5 = (f32[1,4,64,128]{3,2,1,0:T(8,128)S(1)}, f32[1,4,64,128]{3,2,1,0:T(8,128)S(1)}, u32[]{:S(2)}, u32[]{:S(2)}) collective-permute-start(f32[1,4,64,128]{3,2,1,0:T(8,128)S(1)} %slice_add_fusion.12), channel_id=1, source_target_pairs={{0,8},{4,12},{8,0},{12,4},{1,9},{5,13},{9,1},{13,5},{2,10},{6,14},... | collective-permute-start | bytes 393224 | tf_op jit(solution)/shard_map/ppermute | solution.py:147
  40.5 0.0 collective-permute-done.1
  40.5 0.9 %slice_add_fusion.16 = f32[1,4,64,128]{3,2,1,0:T(8,128)S(1)} fusion(f32[2,4,64,128]{3,2,1,0:T(8,128)S(1)} %collective-permute-done.1, f32[4,4,64,128]{3,2,1,0:T(8,128)} %collective-permute-done, f32[4,4,64,128]{3,2,1,0:T(8,128)S(1)} %copy-done.6), kind=kLoop, calls=%fused_computation.26 | loop fusion | flops 65536 | bytes 524288 | tf_op jit(solution)/shard_map/add | solution.py:146
  41.4 1.5 %collective-permute-start.2 = (f32[1,4,64,128]{3,2,1,0:T(8,128)S(1)}, f32[1,4,64,128]{3,2,1,0:T(8,128)S(1)}, u32[]{:S(2)}, u32[]{:S(2)}) collective-permute-start(f32[1,4,64,128]{3,2,1,0:T(8,128)S(1)} %slice_add_fusion.16), channel_id=1, source_target_pairs={{0,8},{4,12},{8,0},{12,4},{1,9},{5,13},{9,1},{13,5},{2,10},{6,14},... | collective-permute-start | bytes 393224 | tf_op jit(solution)/shard_map/ppermute | solution.py:147
  42.9 7.8 %collective-permute-done.5 = f32[1,4,64,128]{3,2,1,0:T(8,128)S(1)} collective-permute-done((f32[1,4,64,128]{3,2,1,0:T(8,128)S(1)}, f32[1,4,64,128]{3,2,1,0:T(8,128)S(1)}, u32[]{:S(2)}, u32[]{:S(2)}) %collective-permute-start.5) | collective-permute-done | bytes 131104 | tf_op jit(solution)/shard_map/ppermute | solution.py:147
  50.7 0.9 %fusion.4 = f32[1,4,64,128]{3,2,1,0:T(8,128)S(1)} fusion(f32[1,4,64,128]{3,2,1,0:T(8,128)S(1)} %collective-permute-done.5, f32[2,4,64,128]{3,2,1,0:T(8,128)S(1)} %collective-permute-done.4, f32[4,4,64,128]{3,2,1,0:T(8,128)} %collective-permute-done.3, f32[4,4,64,128]{3,2,1,0:T(8,128)S(1)} %copy-done.8), kind=kLoop, calls=%fused_computation.24 | loop fusion | flops 98304 | bytes 655360 | tf_op jit(solution)/shard_map/add | solution.py:148
  51.6 0.0 collective-permute-done.7
  51.7 0.4 collective-permute-start.8
  52.1 0.0 collective-permute-done.11
  52.1 1.8 %collective-permute-start.12 = (f32[2,4,64,128]{3,2,1,0:T(8,128)S(1)}, f32[2,4,64,128]{3,2,1,0:T(8,128)S(1)}, u32[]{:S(2)}, u32[]{:S(2)}) collective-permute-start(f32[2,4,64,128]{3,2,1,0:T(8,128)S(1)} %slice_add_fusion), channel_id=1, source_target_pairs={{0,4},{4,0},{8,12},{12,8},{1,5},{5,1},{9,13},{13,9},{2,6},{6,2},{1... | collective-permute-start | bytes 786440 | tf_op jit(solution)/shard_map/ppermute | solution.py:147
  53.9 0.0 collective-permute-done.2
  53.9 0.9 %fusion.5 = f32[1,4,64,128]{3,2,1,0:T(8,128)S(1)} fusion(f32[1,4,64,128]{3,2,1,0:T(8,128)S(1)} %collective-permute-done.2, f32[2,4,64,128]{3,2,1,0:T(8,128)S(1)} %collective-permute-done.1, f32[4,4,64,128]{3,2,1,0:T(8,128)} %collective-permute-done, f32[4,4,64,128]{3,2,1,0:T(8,128)S(1)} %copy-done.6), kind=kLoop, calls=%fused_computation.29 | loop fusion | flops 98304 | bytes 655360 | tf_op jit(solution)/shard_map/add | solution.py:148
  54.8 6.2 %collective-permute-done.8 = f32[2,4,64,128]{3,2,1,0:T(8,128)S(1)} collective-permute-done((f32[2,4,64,128]{3,2,1,0:T(8,128)S(1)}, f32[2,4,64,128]{3,2,1,0:T(8,128)S(1)}, u32[]{:S(2)}, u32[]{:S(2)}) %collective-permute-start.8) | collective-permute-done | bytes 262176 | tf_op jit(solution)/shard_map/ppermute | solution.py:147
  61.0 1.6 %collective-permute-start.9 = (f32[1,4,64,128]{3,2,1,0:T(8,128)S(1)}, f32[1,4,64,128]{3,2,1,0:T(8,128)S(1)}, u32[]{:S(2)}, u32[]{:S(2)}) collective-permute-start(f32[1,4,64,128]{3,2,1,0:T(8,128)S(1)} %slice_add_fusion.8), channel_id=1, source_target_pairs={{0,8},{4,12},{8,0},{12,4},{1,9},{5,13},{9,1},{13,5},{2,10},{6,14},... | collective-permute-start | bytes 393224 | tf_op jit(solution)/shard_map/ppermute | solution.py:147
  62.6 5.1 %collective-permute-done.12 = f32[2,4,64,128]{3,2,1,0:T(8,128)S(1)} collective-permute-done((f32[2,4,64,128]{3,2,1,0:T(8,128)S(1)}, f32[2,4,64,128]{3,2,1,0:T(8,128)S(1)}, u32[]{:S(2)}, u32[]{:S(2)}) %collective-permute-start.12) | collective-permute-done | bytes 262176 | tf_op jit(solution)/shard_map/ppermute | solution.py:147
  67.7 0.7 collective-permute-start.13
  68.5 0.0 collective-permute-done.9
  68.5 6.9 %collective-permute-done.13 = f32[1,4,64,128]{3,2,1,0:T(8,128)S(1)} collective-permute-done((f32[1,4,64,128]{3,2,1,0:T(8,128)S(1)}, f32[1,4,64,128]{3,2,1,0:T(8,128)S(1)}, u32[]{:S(2)}, u32[]{:S(2)}) %collective-permute-start.13) | collective-permute-done | bytes 131104 | tf_op jit(solution)/shard_map/ppermute | solution.py:147
  75.5 0.8 %pad_maximum_fusion = f32[2,8,64,128]{3,2,1,0:T(8,128)} fusion(f32[1,8,64,128]{3,2,1,0:T(8,128)S(1)} %get-tuple-element.24, f32[1,8,64,128]{3,2,1,0:T(8,128)S(1)} %get-tuple-element.23), kind=kLoop, calls=%fused_computation | loop fusion | flops 131072 | bytes 1048576 | tf_op jit(solution)/shard_map/stack | solution.py:152
  (9 shorter events, 0.2 us)
Async XLA Ops:
  0.0 5.3 %copy-start.9 = (s32[3,2]{0,1:T(2,128)S(1)}, s32[3,2]{0,1:T(2,128)}, u32[]{:S(2)}) copy-start(s32[3,2]{0,1:T(2,128)} %param.7) | copy-start | bytes 76
  0.0 5.4 %copy-start = (f32[3,2,128,256]{3,2,1,0:T(8,128)S(1)}, f32[3,2,128,256]{3,2,1,0:T(8,128)}, u32[]{:S(2)}) copy-start(f32[3,2,128,256]{3,2,1,0:T(8,128)} %refs_2_.7) | copy-start | bytes 2359300
  2.4 16.2 %collective-permute-start.6 = (f32[4,256,128]{2,1,0:T(8,128)}, f32[4,256,128]{2,1,0:T(8,128)S(1)}, u32[]{:S(2)}, u32[]{:S(2)}) collective-permute-start(f32[4,256,128]{2,1,0:T(8,128)} %get-tuple-element.21), channel_id=1, source_target_pairs={{0,2},{2,0},{1,3},{3,1},{4,6},{6,4},{5,7},{7,5},{8,10},{10,8},{9,1... | collective-permute-start | bytes 1572872 | tf_op jit(solution)/shard_map/ppermute | solution.py:134
  5.4 1.6 %copy-start.1 = (f32[2,8,256,128]{3,2,1,0:T(8,128)S(1)}, f32[2,8,256,128]{3,2,1,0:T(8,128)}, u32[]{:S(2)}) copy-start(f32[2,8,256,128]{3,2,1,0:T(8,128)} %refs_3_.7) | copy-start | bytes 6291460
  7.0 1.4 %copy-start.3 = (f32[3,2,256,256]{3,2,1,0:T(8,128)S(1)}, f32[3,2,256,256]{3,2,1,0:T(8,128)}, u32[]{:S(2)}) copy-start(f32[3,2,256,256]{3,2,1,0:T(8,128)} %refs_0_.7) | copy-start | bytes 4718596
  12.4 0.8 %copy-start.7 = (f32[4,4,64,128]{3,2,1,0:T(8,128)}, f32[4,4,64,128]{3,2,1,0:T(8,128)S(1)}, u32[]{:S(2)}) copy-start(f32[4,4,64,128]{3,2,1,0:T(8,128)S(1)} %get-tuple-element.15) | copy-start | bytes 1572868
  13.2 5.3 %copy-start.2 = (f32[2,8,256,128]{3,2,1,0:T(8,128)S(1)}, f32[2,8,256,128]{3,2,1,0:T(8,128)}, u32[]{:S(2)}) copy-start(f32[2,8,256,128]{3,2,1,0:T(8,128)} %refs_3_.7) | copy-start | bytes 6291460
  13.2 10.3 %collective-permute-start.3 = (f32[4,4,64,128]{3,2,1,0:T(8,128)}, f32[4,4,64,128]{3,2,1,0:T(8,128)}, u32[]{:S(2)}, u32[]{:S(2)}) collective-permute-start(f32[4,4,64,128]{3,2,1,0:T(8,128)} %get-tuple-element.16), channel_id=1, source_target_pairs={{0,1},{1,0},{2,3},{3,2},{4,5},{5,4},{6,7},{7,6},{8,9},{9,8},{10,11... | collective-permute-start | bytes 1572872 | tf_op jit(solution)/shard_map/ppermute | solution.py:143
  17.1 0.8 %copy-start.5 = (f32[4,4,64,128]{3,2,1,0:T(8,128)}, f32[4,4,64,128]{3,2,1,0:T(8,128)S(1)}, u32[]{:S(2)}) copy-start(f32[4,4,64,128]{3,2,1,0:T(8,128)S(1)} %get-tuple-element.13) | copy-start | bytes 1572868
  17.9 8.7 %collective-permute-start = (f32[4,4,64,128]{3,2,1,0:T(8,128)}, f32[4,4,64,128]{3,2,1,0:T(8,128)}, u32[]{:S(2)}, u32[]{:S(2)}) collective-permute-start(f32[4,4,64,128]{3,2,1,0:T(8,128)} %get-tuple-element.14), channel_id=1, source_target_pairs={{0,1},{1,0},{2,3},{3,2},{4,5},{5,4},{6,7},{7,6},{8,9},{9,8},{10,11... | collective-permute-start | bytes 1572872 | tf_op jit(solution)/shard_map/ppermute | solution.py:143
  18.4 14.1 %collective-permute-start.10 = (f32[4,256,128]{2,1,0:T(8,128)}, f32[4,256,128]{2,1,0:T(8,128)}, u32[]{:S(2)}, u32[]{:S(2)}) collective-permute-start(f32[4,256,128]{2,1,0:T(8,128)} %get-tuple-element.22), channel_id=1, source_target_pairs={{0,2},{2,0},{1,3},{3,1},{4,6},{6,4},{5,7},{7,5},{8,10},{10,8},{9,1... | collective-permute-start | bytes 1572872 | tf_op jit(solution)/shard_map/ppermute | solution.py:134
  18.5 1.4 %copy-start.4 = (f32[3,2,256,256]{3,2,1,0:T(8,128)S(1)}, f32[3,2,256,256]{3,2,1,0:T(8,128)}, u32[]{:S(2)}) copy-start(f32[3,2,256,256]{3,2,1,0:T(8,128)} %refs_0_.7) | copy-start | bytes 4718596
  19.9 3.5 %copy-start.8 = (f32[4,4,64,128]{3,2,1,0:T(8,128)S(1)}, f32[4,4,64,128]{3,2,1,0:T(8,128)}, u32[]{:S(2)}) copy-start(f32[4,4,64,128]{3,2,1,0:T(8,128)} %copy-done.7) | copy-start | bytes 1572868
  19.9 6.7 %copy-start.6 = (f32[4,4,64,128]{3,2,1,0:T(8,128)S(1)}, f32[4,4,64,128]{3,2,1,0:T(8,128)}, u32[]{:S(2)}) copy-start(f32[4,4,64,128]{3,2,1,0:T(8,128)} %copy-done.5) | copy-start | bytes 1572868
  23.3 28.3 %collective-permute-start.7 = (f32[4,4,64,128]{3,2,1,0:T(8,128)S(1)}, f32[4,4,64,128]{3,2,1,0:T(8,128)S(1)}, u32[]{:S(2)}, u32[]{:S(2)}) collective-permute-start(f32[4,4,64,128]{3,2,1,0:T(8,128)S(1)} %get-tuple-element.18), channel_id=1, source_target_pairs={{0,1},{1,0},{2,3},{3,2},{4,5},{5,4},{6,7},{7,6},{8,9},{9,8},{10,11... | collective-permute-start | bytes 1572872 | tf_op jit(solution)/shard_map/ppermute | solution.py:143
  24.4 12.5 %collective-permute-start.4 = (f32[2,4,64,128]{3,2,1,0:T(8,128)S(1)}, f32[2,4,64,128]{3,2,1,0:T(8,128)S(1)}, u32[]{:S(2)}, u32[]{:S(2)}) collective-permute-start(f32[2,4,64,128]{3,2,1,0:T(8,128)S(1)} %slice_add_fusion.2), channel_id=1, source_target_pairs={{0,4},{4,0},{8,12},{12,8},{1,5},{5,1},{9,13},{13,9},{2,6},{6,2},{1... | collective-permute-start | bytes 786440 | tf_op jit(solution)/shard_map/ppermute | solution.py:147
  27.6 12.9 %collective-permute-start.1 = (f32[2,4,64,128]{3,2,1,0:T(8,128)S(1)}, f32[2,4,64,128]{3,2,1,0:T(8,128)S(1)}, u32[]{:S(2)}, u32[]{:S(2)}) collective-permute-start(f32[2,4,64,128]{3,2,1,0:T(8,128)S(1)} %slice_add_fusion.3), channel_id=1, source_target_pairs={{0,4},{4,0},{8,12},{12,8},{1,5},{5,1},{9,13},{13,9},{2,6},{6,2},{1... | collective-permute-start | bytes 786440 | tf_op jit(solution)/shard_map/ppermute | solution.py:147
  36.8 15.3 %collective-permute-start.11 = (f32[4,4,64,128]{3,2,1,0:T(8,128)S(1)}, f32[4,4,64,128]{3,2,1,0:T(8,128)S(1)}, u32[]{:S(2)}, u32[]{:S(2)}) collective-permute-start(f32[4,4,64,128]{3,2,1,0:T(8,128)S(1)} %get-tuple-element.20), channel_id=1, source_target_pairs={{0,1},{1,0},{2,3},{3,2},{4,5},{5,4},{6,7},{7,6},{8,9},{9,8},{10,11... | collective-permute-start | bytes 1572872 | tf_op jit(solution)/shard_map/ppermute | solution.py:143
  37.8 12.9 %collective-permute-start.5 = (f32[1,4,64,128]{3,2,1,0:T(8,128)S(1)}, f32[1,4,64,128]{3,2,1,0:T(8,128)S(1)}, u32[]{:S(2)}, u32[]{:S(2)}) collective-permute-start(f32[1,4,64,128]{3,2,1,0:T(8,128)S(1)} %slice_add_fusion.12), channel_id=1, source_target_pairs={{0,8},{4,12},{8,0},{12,4},{1,9},{5,13},{9,1},{13,5},{2,10},{6,14},... | collective-permute-start | bytes 393224 | tf_op jit(solution)/shard_map/ppermute | solution.py:147
  41.4 12.5 %collective-permute-start.2 = (f32[1,4,64,128]{3,2,1,0:T(8,128)S(1)}, f32[1,4,64,128]{3,2,1,0:T(8,128)S(1)}, u32[]{:S(2)}, u32[]{:S(2)}) collective-permute-start(f32[1,4,64,128]{3,2,1,0:T(8,128)S(1)} %slice_add_fusion.16), channel_id=1, source_target_pairs={{0,8},{4,12},{8,0},{12,4},{1,9},{5,13},{9,1},{13,5},{2,10},{6,14},... | collective-permute-start | bytes 393224 | tf_op jit(solution)/shard_map/ppermute | solution.py:147
  51.7 9.3 %collective-permute-start.8 = (f32[2,4,64,128]{3,2,1,0:T(8,128)S(1)}, f32[2,4,64,128]{3,2,1,0:T(8,128)S(1)}, u32[]{:S(2)}, u32[]{:S(2)}) collective-permute-start(f32[2,4,64,128]{3,2,1,0:T(8,128)S(1)} %slice_add_fusion.1), channel_id=1, source_target_pairs={{0,4},{4,0},{8,12},{12,8},{1,5},{5,1},{9,13},{13,9},{2,6},{6,2},{1... | collective-permute-start | bytes 786440 | tf_op jit(solution)/shard_map/ppermute | solution.py:147
  52.1 15.6 %collective-permute-start.12 = (f32[2,4,64,128]{3,2,1,0:T(8,128)S(1)}, f32[2,4,64,128]{3,2,1,0:T(8,128)S(1)}, u32[]{:S(2)}, u32[]{:S(2)}) collective-permute-start(f32[2,4,64,128]{3,2,1,0:T(8,128)S(1)} %slice_add_fusion), channel_id=1, source_target_pairs={{0,4},{4,0},{8,12},{12,8},{1,5},{5,1},{9,13},{13,9},{2,6},{6,2},{1... | collective-permute-start | bytes 786440 | tf_op jit(solution)/shard_map/ppermute | solution.py:147
  61.0 7.4 %collective-permute-start.9 = (f32[1,4,64,128]{3,2,1,0:T(8,128)S(1)}, f32[1,4,64,128]{3,2,1,0:T(8,128)S(1)}, u32[]{:S(2)}, u32[]{:S(2)}) collective-permute-start(f32[1,4,64,128]{3,2,1,0:T(8,128)S(1)} %slice_add_fusion.8), channel_id=1, source_target_pairs={{0,8},{4,12},{8,0},{12,4},{1,9},{5,13},{9,1},{13,5},{2,10},{6,14},... | collective-permute-start | bytes 393224 | tf_op jit(solution)/shard_map/ppermute | solution.py:147
  67.7 7.7 %collective-permute-start.13 = (f32[1,4,64,128]{3,2,1,0:T(8,128)S(1)}, f32[1,4,64,128]{3,2,1,0:T(8,128)S(1)}, u32[]{:S(2)}, u32[]{:S(2)}) collective-permute-start(f32[1,4,64,128]{3,2,1,0:T(8,128)S(1)} %slice_add_fusion.4), channel_id=1, source_target_pairs={{0,8},{4,12},{8,0},{12,4},{1,9},{5,13},{9,1},{13,5},{2,10},{6,14},... | collective-permute-start | bytes 393224 | tf_op jit(solution)/shard_map/ppermute | solution.py:147

commit v2 on v0

v2 whole, which is shorter than its diff:
```python
import functools

import jax
import jax.numpy as jnp
from jax import lax
from jax.experimental import pallas as pl
from jax.experimental.pallas import tpu as pltpu
from jax.sharding import PartitionSpec as P

CHUNKS = 2
ANY = pl.BlockSpec(memory_space=pl.ANY)
VMEM = pl.BlockSpec(memory_space=pltpu.VMEM)


def halving_order(peers):
    bits = peers.bit_length() - 1
    assert peers == 1 << bits
    return sorted(range(peers), key=lambda m: -sum(((m >> b) & 1) << (bits - 1 - b) for b in range(bits)))


def halves(value):
    high = value.astype(jnp.bfloat16)
    return high, (value - high.astype(jnp.float32)).astype(jnp.bfloat16)


def pinned(space, *values):
    return [pltpu.with_memory_space_constraint(value, space) for value in values]


def edge_kernel(count, scalars, psi, earlier, *refs):
    edges, sem = refs[:-1], refs[-1]
    copies = [
        pltpu.make_async_copy(psi.at[scalars[0], pl.ds(c * count, count)], edge, sem.at[c]) for c, edge in enumerate(edges)
    ]
    for copy in copies:
        copy.start()
    for copy in copies:
        copy.wait()


def edges_of(sector, psi, count, earlier):
    chunks = psi.shape[1] // count
    edge = jax.ShapeDtypeStruct((count,) + psi.shape[2:], psi.dtype)
    return pl.pallas_call(
        functools.partial(edge_kernel, count),
        out_shape=[edge] * chunks,
        in_specs=[pl.BlockSpec(memory_space=pltpu.SMEM), pl.BlockSpec(memory_space=pltpu.HBM), ANY],
        out_specs=[VMEM] * chunks,
        scratch_shapes=[pltpu.SemaphoreType.DMA((chunks,))],
        compiler_params=pltpu.CompilerParams(vmem_limit_bytes=1024 * 1024),
        name="edges",
    )(jnp.reshape(sector, (1,)), *pinned(pltpu.HBM, psi), earlier)


def relay_kernel(value, earlier, out):
    pass


def relay(value, earlier):
    return pl.pallas_call(
        relay_kernel,
        out_shape=jax.ShapeDtypeStruct(value.shape, value.dtype),
        in_specs=[ANY, ANY],
        out_specs=ANY,
        input_output_aliases={0: 0},
        compiler_params=pltpu.CompilerParams(vmem_limit_bytes=1024 * 1024),
        name="relay",
    )(value, earlier)


def stage_kernel(order, scalars, left, left_cat):
    terms, rows, depth = left.shape[0], left.shape[2], left.shape[3]
    piece = rows // len(order)
    for t in range(terms):
        ordered = [left[t, 0, pl.ds(pl.multiple_of((scalars[0] ^ m) * piece, piece), piece), :] for m in order]
        high, low = halves(jnp.concatenate(ordered, axis=0))
        start = t * 3 * depth
        left_cat[0, :, start:start + depth] = high
        left_cat[0, :, start + depth:start + 2 * depth] = high
        left_cat[0, :, start + 2 * depth:start + 3 * depth] = low


def staged(place, left, order):
    terms, sectors, rows, depth = left.shape
    return pl.pallas_call(
        functools.partial(stage_kernel, order),
        out_shape=jax.ShapeDtypeStruct((sectors, rows, terms * 3 * depth), jnp.bfloat16),
        grid_spec=pltpu.PrefetchScalarGridSpec(
            num_scalar_prefetch=1,
            grid=(sectors,),
            in_specs=[pl.BlockSpec((terms, 1, rows, depth), lambda i, s: (0, i, 0, 0))],
            out_specs=pl.BlockSpec((1, rows, terms * 3 * depth), lambda i, s: (i, 0, 0)),
        ),
        compiler_params=pltpu.CompilerParams(vmem_limit_bytes=16 * 1024 * 1024),
        name="stage",
    )(jnp.reshape(place, (1,)), *pinned(pltpu.HBM, left))


def summed(addends, size, earlier):
    def kernel(*refs):
        pieces = [ref[start:start + size] for ref, (array, start) in zip(refs, addends)]
        refs[-1][...] = functools.reduce(lambda a, b: a + b, pieces)

    return pl.pallas_call(
        kernel,
        out_shape=jax.ShapeDtypeStruct((size,) + addends[0][0].shape[1:], jnp.float32),
        in_specs=[VMEM] * len(addends) + [ANY] * len(earlier),
        out_specs=VMEM,
        compiler_params=pltpu.CompilerParams(vmem_limit_bytes=4 * 1024 * 1024),
        name="summed",
    )(*[array for array, start in addends], *earlier)


def gather_kernel(counts, scalars, *refs):
    out, at = refs[-1], 0
    for which, first, starts in counts:
        total = functools.reduce(lambda a, b: a + b, [ref[start] for ref, start in zip(refs[at:], starts)])
        out[scalars[which], first:first + total.shape[0]] = total
        at += len(starts)


def gathered(targets, items, shape):
    addends = [addend for item in items.values() for addend in item]

    return pl.pallas_call(
        functools.partial(gather_kernel, [(*item, [start for array, start in each]) for item, each in items.items()]),
        out_shape=jax.ShapeDtypeStruct(shape, jnp.float32),
        in_specs=[pl.BlockSpec(memory_space=pltpu.SMEM)] + [VMEM] * len(addends),
        out_specs=VMEM,
        compiler_params=pltpu.CompilerParams(vmem_limit_bytes=8 * 1024 * 1024),
        name="gathered",
    )(jnp.stack(targets), *[array for array, start in addends])


def chunk_kernel(order, terms, first, count, with_halo, scalars, left_cat, *refs):
    rights, psis, halos = refs[:2], refs[2:4], refs[4:4 + 2 * with_halo]
    sent, kept, left_in, right_in, psi_in, right_cat, psi_cat, mid_cat, sem = refs[-9:]
    depth, width = psis[0].shape[2:]
    columns = right_in.shape[3]
    piece = left_in.shape[0] // len(order)
    sources = 2 + with_halo
    target, here = scalars[0], pl.ds(pl.multiple_of(scalars[1] * columns, columns), columns)

    right_copies = [pltpu.make_async_copy(rights[at].at[:, target, :, here], right_in.at[at], sem.at[at]) for at in range(2)]
    psi_copies = {}
    for source in range(sources):
        for at in range(2):
            origin = psis[at].at[source, pl.ds(first, count)] if source < 2 else halos[at]
            psi_copies[source, at] = pltpu.make_async_copy(origin, psi_in.at[source, at], sem.at[2 + 2 * source + at])
    left_copy = pltpu.make_async_copy(left_cat.at[target], left_in, sem.at[2 + 2 * sources])
    for copy in right_copies + list(psi_copies.values()) + [left_copy]:
        copy.start()

    for at in range(2):
        right_copies[at].wait()
        for t in range(terms):
            high, low = halves(right_in[at, t])
            for again in (at * width, (at + 2) * width):
                right_cat[t, again:again + width, 0:columns] = high
                right_cat[t, again:again + width, columns:2 * columns] = low
    for source in range(sources):
        for at in range(2):
            psi_copies[source, at].wait()
            for v in range(count):
                high, low = halves(psi_in[source, at, v])
                psi_cat[source, v * depth:(v + 1) * depth, at * width:(at + 1) * width] = high
                psi_cat[source, v * depth:(v + 1) * depth, (2 + at) * width:(3 + at) * width] = low
    for t in range(terms):
        mid = jnp.dot(psi_cat[scalars[2 + t]], right_cat[t], preferred_element_type=jnp.float32)
        high, low = halves(mid[:, 0:columns] + mid[:, columns:2 * columns])
        for v in range(count):
            start = t * 3 * depth
            mid_cat[start:start + depth, v * columns:(v + 1) * columns] = high[v * depth:(v + 1) * depth]
            mid_cat[start + depth:start + 2 * depth, v * columns:(v + 1) * columns] = low[v * depth:(v + 1) * depth]
            mid_cat[start + 2 * depth:start + 3 * depth, v * columns:(v + 1) * columns] = high[v * depth:(v + 1) * depth]
    left_copy.wait()
    total = jnp.dot(left_in[...], mid_cat[...], preferred_element_type=jnp.float32)
    half = len(order) // 2
    for v in range(count):
        for p in range(len(order)):
            ref = sent if p < half else kept
            ref[p % half, v] = total[p * piece:(p + 1) * piece, v * columns:(v + 1) * columns]


def chunk(scalars, left_cat, rights, psis, halos, first, count, order, earlier=()):
    rows = left_cat.shape[1]
    depth, width = psis[0].shape[2:]
    terms, columns = rights[0].shape[0], rights[0].shape[3] // 2
    with_halo = halos is not None
    args = pinned(pltpu.HBM, left_cat, rights[0]) + [rights[1]] + pinned(pltpu.HBM, psis[0]) + [psis[1], *(halos or ()), *earlier]
    out = jax.ShapeDtypeStruct((len(order) // 2, count, rows // len(order), columns), jnp.float32)
    flops = 2 * 3 * terms * count * rows * columns * (depth + 2 * width)
    sources = 2 + with_halo
    return pl.pallas_call(
        functools.partial(chunk_kernel, order, terms, first, count, with_halo),
        out_shape=(out, out),
        in_specs=[pl.BlockSpec(memory_space=pltpu.SMEM)] + [ANY] * len(args),
        out_specs=(VMEM,) * 2,
        scratch_shapes=[
            pltpu.VMEM((rows, terms * 3 * depth), jnp.bfloat16),
            pltpu.VMEM((2, terms, width, columns), jnp.float32),
            pltpu.VMEM((sources, 2, count, depth, width), jnp.float32),
            pltpu.VMEM((terms, 4 * width, 2 * columns), jnp.bfloat16),
            pltpu.VMEM((sources, count * depth, 4 * width), jnp.bfloat16),
            pltpu.VMEM((terms * 3 * depth, count * columns), jnp.bfloat16),
            pltpu.SemaphoreType.DMA((3 + 2 * sources,)),
        ],
        compiler_params=pltpu.CompilerParams(vmem_limit_bytes=20 * 1024 * 1024),
        cost_estimate=pl.CostEstimate(flops=flops, bytes_accessed=8 * 1024 * 1024, transcendentals=0),
        name="terms_of_sector",
    )(scalars, *args)


def shards(wavefunction, left_operators, right_operators, source_sectors):
    sectors, vectors = wavefunction.shape[:2]
    assert sectors == 2
    peers, places = lax.axis_size("term"), lax.axis_size("sec")
    z, x, core = lax.axis_index("term"), lax.axis_index("sec"), lax.axis_index("sub")
    order = halving_order(peers)
    stages = [[(i, i ^ (1 << b)) for i in range(peers)] for b in range(peers.bit_length() - 1)]
    swap = [(0, 1), (1, 0)]
    relative = source_sectors - x * sectors
    picks = jnp.where((relative >= 0) & (relative < sectors), relative, 2)
    count = vectors // CHUNKS
    psis = [wavefunction, lax.ppermute(wavefunction, "sub", swap)]
    rights = [right_operators, lax.ppermute(right_operators, "sub", swap)]
    left_cat = staged(z, left_operators, order)

    targets = (x, 1 - x) if places == 2 else (jnp.int32(0), jnp.int32(1))

    if places == 2:
        ways = [None, (targets[1], swap)]
    else:
        up = [(i, i + 1) for i in range(places - 1)]
        ways = [(jnp.int32(1), up), (jnp.int32(0), [(j, i) for i, j in up])]
    halos = {}
    for which in range(2):
        if ways[which] is not None:
            edges = edges_of(ways[which][0], wavefunction, count, left_cat)
            for c, edge in enumerate(edges):
                halos[which, c * count] = lax.ppermute(edge, "sec", ways[which][1])

    def compute(item, earlier):
        which, first = item
        sources = lax.dynamic_index_in_dim(picks, targets[which], 1, keepdims=False)
        both = None
        if item in halos:
            halo = halos[item] if earlier is None else relay(halos[item], earlier)
            both = [halo, lax.ppermute(halo, "sub", swap)]
        else:
            sources = jnp.minimum(sources, 1)
        scalars = jnp.concatenate([jnp.stack([targets[which], core]), sources])
        return chunk(scalars, left_cat, rights, psis, both, first, count, order, [] if earlier is None else [earlier])

    work = [(which, first) for which in range(2) for first in range(0, vectors, count)]
    parts, last, newest = {}, None, None
    for at in range(len(work) + len(stages) - 1):
        if at < len(work):
            item = work[at]
            newest, kept = compute(item, last)
            parts[item] = [(kept, 0), (lax.ppermute(newest, "term", stages[0]), 0)]
        for stage in range(1, len(stages)):
            if 0 <= at - stage < len(work):
                item = work[at - stage]
                half = peers >> (stage + 1)
                behind = parts[work[at - stage - 1]][-1:] if at > stage else []
                last = summed(parts[item], half, [newest] + [array for array, start in behind])
                parts[item] = [(array, start + half) for array, start in parts[item]]
                parts[item].append((lax.ppermute(last, "term", stages[stage]), 0))
    return gathered(targets, parts, (sectors, vectors) + parts[work[0]][0][0].shape[2:])


def solution(mesh):
    in_specs = (
        P(("grp", "sec"), None, None, "sub"),
        P("term", ("grp", "sec"), None, None),
        P("term", ("grp", "sec"), "sub", None),
        P("term", ("grp", "sec")),
    )
    out_specs = P(("grp", "sec"), None, "term", "sub")
    return jax.shard_map(shards, mesh=mesh, in_specs=in_specs, out_specs=out_specs, check_vma=False)
```

time: 180 us -> 66 us (0.37)
  waiting for transfers between devices: 114 us -> 20.4 us
  matrix products: 24.8 us -> 0 us
  Pallas kernels: 0 us -> 22.5 us
  local copies, waits for them, and re-layouts: 16.4 us -> 0.8 us
  starting transfers between devices: 7.19 us -> 21.6 us
  between operations: 13.4 us -> 0.13 us
  other arithmetic: 4.66 us -> 0.24 us
    reduce_scatter x2 -> x0, waiting for transfers between devices: 88.6 us -> none  [the longest x1 77.2 us: shards(): lax.psum_scatter(partial_sum, 'term', scatter_dimension=2, tiled=True)]
    dot_general x2 -> x0, matrix products: 24.8 us -> none  [the longest x1 12.9 us: shards(): jnp.einsum('tsvjk,tskl->tsvjl', picked, right_operators, precision=highest)]
    pallas_call x0 -> x13, Pallas kernels: none -> 22.5 us  [the longest x4 16.7 us: chunk(): pl.pallas_call(functools.partial(chunk_kernel, order, terms, first, count...]
    ppermute x2 -> x14, starting transfers between devices: 7.15 us -> 21.6 us  [the longest x4 10.8 us: shards(): parts[item].append((lax.ppermute(last, 'term', stages[stage]), 0))]
    gather x1 -> x0, local copies, waits for them, and re-layouts: 5.87 us -> none  [shards(): picked = jnp.take(padded, relative, axis=0)]
    transpose x1 -> x0, local copies, waits for them, and re-layouts: 5.49 us -> none  [shards(): jnp.einsum('tsij,tsvjl->svil', left_operators, middle, precision=highest)]
    ppermute x2 -> x14, waiting for transfers between devices: 25.1 us -> 20.4 us  [the longest x4 12.7 us: shards(): parts[item].append((lax.ppermute(last, 'term', stages[stage]), 0))]
    concatenate x1 -> x2, other arithmetic: 4.64 us -> 0.15 us  [compute(): scalars = jnp.concatenate([jnp.stack([targets[which], core]), sources])]
  transfers between devices with their start and end apart: 4 -> 14, of which waited for: 4 -> 9; matrix products, arithmetic and copies ran while one was open for 0% -> 0% of each run, Pallas kernels for 0% -> 32%
where the time goes in v2:
time: 66 us; the launch traced here: 65.7 us
  Pallas kernels  22.5 us (34%)
  starting transfers between devices  21.6 us (33%)
  waiting for transfers between devices  20.4 us (31%)
  local copies, waits for them, and re-layouts  0.8 us (1%)
    pallas_call x4, Pallas kernels, chunk(): pl.pallas_call(functools.partial(chunk_kernel, order, terms, first, count...  16.7 us
    ppermute x4, waiting for transfers between devices, shards(): parts[item].append((lax.ppermute(last, 'term', stages[stage]), 0))  12.7 us
    ppermute x4, starting transfers between devices, shards(): parts[item].append((lax.ppermute(last, 'term', stages[stage]), 0))  10.8 us
    ppermute x4, waiting for transfers between devices, shards(): parts[item] = [(kept, 0), (lax.ppermute(newest, 'term', stages[0]), 0)]  6.26 us
    ppermute x4, starting transfers between devices, shards(): parts[item] = [(kept, 0), (lax.ppermute(newest, 'term', stages[0]), 0)]  5.55 us
    ppermute x2, starting transfers between devices, shards(): halos[which, c * count] = lax.ppermute(edge, 'sec', ways[which][1])  4.67 us
    pallas_call x1, Pallas kernels, edges_of(): pl.pallas_call(functools.partial(edge_kernel, count), out_shape=[edge] *...  2.82 us
    pallas_call x1, Pallas kernels, staged(): pl.pallas_call(functools.partial(stage_kernel, order), out_shape=jax.Shap...  1.53 us
  transfers between devices with their start and end apart: 14, of which 9 were waited for; matrix products, arithmetic and copies ran while one was open for 0% of the time, Pallas kernels for 32%

profile of v2, /device:TPU:0, one launch (start us, length us, event | category | flops | bytes accessed | tf_op | source)
XLA Modules:
  0.0 65.7 jit_solution(15352638804176526184)
XLA Ops:
  0.0 0.5 collective-permute-start.1
  0.5 0.1 collective-permute-start
  0.5 1.5 %stage.1.left_cat.earlier = bf16[2,256,2304]{2,1,0:T(8,128)(2,1)S(1)} custom-call(s32[1]{0:T(128)} %bitcast.4.scalars, f32[3,2,256,256]{3,2,1,0:T(8,128)} %left.1), custom_call_target="tpu_custom_call" | custom-call | tf_op jit(solution)/shard_map/stage/pallas_call | solution.py:85
  2.0 0.0 copy-start
  2.1 0.0 copy-start.3
  2.1 2.8 %edges.1 = (f32[4,256,128]{2,1,0:T(8,128)}, f32[4,256,128]{2,1,0:T(8,128)S(1)}) custom-call(s32[1]{0:T(128)} %bitcast.1.scalars, f32[2,8,256,128]{3,2,1,0:T(8,128)} %refs_2_.7, bf16[2,256,2304]{2,1,0:T(8,128)(2,1)S(1)} %stage.1.left_cat.earlier), custom_call_target="tpu_custom_call" | custom-call | tf_op jit(solution)/shard_map/edges/pallas_call | solution.py:44
  4.9 0.0 copy-done
  4.9 0.0 copy-start.1
  4.9 0.8 %copy-done.1 = f32[4,256,128]{2,1,0:T(8,128)} copy-done((f32[4,256,128]{2,1,0:T(8,128)}, f32[4,256,128]{2,1,0:T(8,128)S(1)}, u32[]{:S(2)}) %copy-start.1) | copy-done | bytes 524312
  5.7 2.9 %collective-permute-start.5 = (f32[4,256,128]{2,1,0:T(8,128)}, f32[4,256,128]{2,1,0:T(8,128)S(1)}, u32[]{:S(2)}, u32[]{:S(2)}) collective-permute-start(f32[4,256,128]{2,1,0:T(8,128)} %get-tuple-element.19), channel_id=1, source_target_pairs={{0,2},{2,0},{1,3},{3,1},{4,6},{6,4},{5,7},{7,5},{8,10},{10,8},{9,1... | collective-permute-start | bytes 1572872 | tf_op jit(solution)/shard_map/ppermute | solution.py:241
  8.6 0.0 copy-done.3
  8.7 0.1 pad_add_fusion.1.scalars
  8.7 0.0 collective-permute-done.refs_1_
  8.7 0.0 collective-permute-done.1.refs_3_
  8.7 4.1 %terms_of_sector.4 = (f32[2,4,64,128]{3,2,1,0:T(8,128)S(1)}, f32[2,4,64,128]{3,2,1,0:T(8,128)S(1)}) custom-call(s32[5]{0:T(128)S(1)} %pad_add_fusion.1.scalars, bf16[2,256,2304]{2,1,0:T(8,128)(2,1)} %copy-done, f32[3,2,128,256]{3,2,1,0:T(8,128)} %refs_0_.7, f32[3,2,128,256]{3,2,1,0:T(8,128)S(1)} %collective-permute-done.refs_1_, f32[2,8,256,128]{3,2,1,0:T(8,128)} %refs_2_.7, ...), custom_call_target="tpu_custom_call" | custom-call | flops 1207959552 | bytes 8388608 | tf_op jit(solution)/shard_map/terms_of_sector/pallas_call | solution.py:194
  12.8 1.6 %collective-permute-start.2 = (f32[2,4,64,128]{3,2,1,0:T(8,128)S(1)}, f32[2,4,64,128]{3,2,1,0:T(8,128)S(1)}, u32[]{:S(2)}, u32[]{:S(2)}) collective-permute-start(f32[2,4,64,128]{3,2,1,0:T(8,128)S(1)} %get-tuple-element.16), channel_id=1, source_target_pairs={{0,4},{4,0},{8,12},{12,8},{1,5},{5,1},{9,13},{13,9},{2,6},{6,2},{1... | collective-permute-start | bytes 786440 | tf_op jit(solution)/shard_map/ppermute | solution.py:261
  14.5 4.1 %terms_of_sector.5 = (f32[2,4,64,128]{3,2,1,0:T(8,128)S(1)}, f32[2,4,64,128]{3,2,1,0:T(8,128)S(1)}) custom-call(s32[5]{0:T(128)S(1)} %pad_add_fusion.1.scalars, bf16[2,256,2304]{2,1,0:T(8,128)(2,1)} %copy-done, f32[3,2,128,256]{3,2,1,0:T(8,128)} %refs_0_.7, f32[3,2,128,256]{3,2,1,0:T(8,128)S(1)} %collective-permute-done.refs_1_, f32[2,8,256,128]{3,2,1,0:T(8,128)} %refs_2_.7, ...), custom_call_target="tpu_custom_call" | custom-call | flops 1207959552 | bytes 8388608 | tf_op jit(solution)/shard_map/terms_of_sector/pallas_call | solution.py:194
  18.6 0.0 copy-start.2
  18.6 2.3 %collective-permute-done.2.refs_1_ = f32[2,4,64,128]{3,2,1,0:T(8,128)S(1)} collective-permute-done((f32[2,4,64,128]{3,2,1,0:T(8,128)S(1)}, f32[2,4,64,128]{3,2,1,0:T(8,128)S(1)}, u32[]{:S(2)}, u32[]{:S(2)}) %collective-permute-start.2) | collective-permute-done | bytes 262176 | tf_op jit(solution)/shard_map/ppermute | solution.py:261
  20.9 0.1 collective-permute-done.5.value
  20.9 0.0 collective-permute-start.6
  21.0 0.0 copy-done.2
  21.0 1.7 %collective-permute-start.9 = (f32[4,256,128]{2,1,0:T(8,128)S(1)}, f32[4,256,128]{2,1,0:T(8,128)S(1)}, u32[]{:S(2)}, u32[]{:S(2)}) collective-permute-start(f32[4,256,128]{2,1,0:T(8,128)S(1)} %copy-done.2), channel_id=1, source_target_pairs={{0,2},{2,0},{1,3},{3,1},{4,6},{6,4},{5,7},{7,5},{8,10},{10,8},{9,1... | collective-permute-start | bytes 1572872 | tf_op jit(solution)/shard_map/ppermute | solution.py:241
  22.7 1.6 %collective-permute-start.4 = (f32[2,4,64,128]{3,2,1,0:T(8,128)S(1)}, f32[2,4,64,128]{3,2,1,0:T(8,128)S(1)}, u32[]{:S(2)}, u32[]{:S(2)}) collective-permute-start(f32[2,4,64,128]{3,2,1,0:T(8,128)S(1)} %get-tuple-element.17.refs_2_), channel_id=1, source_target_pairs={{0,4},{4,0},{8,12},{12,8},{1,5},{5,1},{9,13},{13,9},{2,6},{6,2},{1... | collective-permute-start | bytes 786440 | tf_op jit(solution)/shard_map/ppermute | solution.py:261
  24.3 2.6 %collective-permute-start.3 = (f32[1,4,64,128]{3,2,1,0:T(8,128)S(1)}, f32[1,4,64,128]{3,2,1,0:T(8,128)S(1)}, u32[]{:S(2)}, u32[]{:S(2)}) collective-permute-start(f32[1,4,64,128]{3,2,1,0:T(8,128)S(1)} %summed.4.earlier.refs_6_), channel_id=1, source_target_pairs={{0,8},{4,12},{8,0},{12,4},{1,9},{5,13},{9,1},{13,5},{2,10},{6,14},... | collective-permute-start | bytes 393224 | tf_op jit(solution)/shard_map/ppermute | solution.py:269
  26.9 0.1 pad_add_fusion.2.scalars
  26.9 0.0 collective-permute-done.6.refs_5_
  26.9 4.3 %terms_of_sector.6 = (f32[2,4,64,128]{3,2,1,0:T(8,128)S(1)}, f32[2,4,64,128]{3,2,1,0:T(8,128)S(1)}) custom-call(s32[5]{0:T(128)S(1)} %pad_add_fusion.2.scalars, bf16[2,256,2304]{2,1,0:T(8,128)(2,1)} %copy-done, f32[3,2,128,256]{3,2,1,0:T(8,128)} %refs_0_.7, f32[3,2,128,256]{3,2,1,0:T(8,128)S(1)} %collective-permute-done.refs_1_, f32[2,8,256,128]{3,2,1,0:T(8,128)} %refs_2_.7, ...), custom_call_target="tpu_custom_call" | custom-call | flops 1207959552 | bytes 8388608 | tf_op jit(solution)/shard_map/terms_of_sector/pallas_call | solution.py:194
  31.2 2.7 %collective-permute-done.4.refs_1_.refs_4_ = f32[2,4,64,128]{3,2,1,0:T(8,128)S(1)} collective-permute-done((f32[2,4,64,128]{3,2,1,0:T(8,128)S(1)}, f32[2,4,64,128]{3,2,1,0:T(8,128)S(1)}, u32[]{:S(2)}, u32[]{:S(2)}) %collective-permute-start.4) | collective-permute-done | bytes 262176 | tf_op jit(solution)/shard_map/ppermute | solution.py:261
  33.9 0.0 collective-permute-done.3.refs_3_.refs_2_
  34.0 1.3 %collective-permute-done.9.value = f32[4,256,128]{2,1,0:T(8,128)S(1)} collective-permute-done((f32[4,256,128]{2,1,0:T(8,128)S(1)}, f32[4,256,128]{2,1,0:T(8,128)S(1)}, u32[]{:S(2)}, u32[]{:S(2)}) %collective-permute-start.9) | collective-permute-done | bytes 524320 | tf_op jit(solution)/shard_map/ppermute | solution.py:241
  35.3 0.0 collective-permute-start.10
  35.3 1.8 %collective-permute-start.8 = (f32[2,4,64,128]{3,2,1,0:T(8,128)S(1)}, f32[2,4,64,128]{3,2,1,0:T(8,128)S(1)}, u32[]{:S(2)}, u32[]{:S(2)}) collective-permute-start(f32[2,4,64,128]{3,2,1,0:T(8,128)S(1)} %get-tuple-element.20.refs_2_), channel_id=1, source_target_pairs={{0,4},{4,0},{8,12},{12,8},{1,5},{5,1},{9,13},{13,9},{2,6},{6,2},{1... | collective-permute-start | bytes 786440 | tf_op jit(solution)/shard_map/ppermute | solution.py:261
  37.1 2.6 %collective-permute-start.7 = (f32[1,4,64,128]{3,2,1,0:T(8,128)S(1)}, f32[1,4,64,128]{3,2,1,0:T(8,128)S(1)}, u32[]{:S(2)}, u32[]{:S(2)}) collective-permute-start(f32[1,4,64,128]{3,2,1,0:T(8,128)S(1)} %summed.5.earlier.refs_6_), channel_id=1, source_target_pairs={{0,8},{4,12},{8,0},{12,4},{1,9},{5,13},{9,1},{13,5},{2,10},{6,14},... | collective-permute-start | bytes 393224 | tf_op jit(solution)/shard_map/ppermute | solution.py:269
  39.7 0.0 collective-permute-done.10.refs_5_
  39.7 4.3 %terms_of_sector.7 = (f32[2,4,64,128]{3,2,1,0:T(8,128)S(1)}, f32[2,4,64,128]{3,2,1,0:T(8,128)S(1)}) custom-call(s32[5]{0:T(128)S(1)} %pad_add_fusion.2.scalars, bf16[2,256,2304]{2,1,0:T(8,128)(2,1)} %copy-done, f32[3,2,128,256]{3,2,1,0:T(8,128)} %refs_0_.7, f32[3,2,128,256]{3,2,1,0:T(8,128)S(1)} %collective-permute-done.refs_1_, f32[2,8,256,128]{3,2,1,0:T(8,128)} %refs_2_.7, ...), custom_call_target="tpu_custom_call" | custom-call | flops 1207959552 | bytes 8388608 | tf_op jit(solution)/shard_map/terms_of_sector/pallas_call | solution.py:194
  44.0 0.5 collective-permute-start.12
  44.5 2.0 %collective-permute-done.7.refs_3_.refs_5_ = f32[1,4,64,128]{3,2,1,0:T(8,128)S(1)} collective-permute-done((f32[1,4,64,128]{3,2,1,0:T(8,128)S(1)}, f32[1,4,64,128]{3,2,1,0:T(8,128)S(1)}, u32[]{:S(2)}, u32[]{:S(2)}) %collective-permute-start.7) | collective-permute-done | bytes 131104 | tf_op jit(solution)/shard_map/ppermute | solution.py:269
  46.6 0.6 collective-permute-done.8.refs_1_.refs_7_
  47.2 2.9 %collective-permute-start.11 = (f32[1,4,64,128]{3,2,1,0:T(8,128)S(1)}, f32[1,4,64,128]{3,2,1,0:T(8,128)S(1)}, u32[]{:S(2)}, u32[]{:S(2)}) collective-permute-start(f32[1,4,64,128]{3,2,1,0:T(8,128)S(1)} %summed.6), channel_id=1, source_target_pairs={{0,8},{4,12},{8,0},{12,4},{1,9},{5,13},{9,1},{13,5},{2,10},{6,14},... | collective-permute-start | bytes 393224 | tf_op jit(solution)/shard_map/ppermute | solution.py:269
  50.0 4.6 %collective-permute-done.11.refs_3_.refs_8_ = f32[1,4,64,128]{3,2,1,0:T(8,128)S(1)} collective-permute-done((f32[1,4,64,128]{3,2,1,0:T(8,128)S(1)}, f32[1,4,64,128]{3,2,1,0:T(8,128)S(1)}, u32[]{:S(2)}, u32[]{:S(2)}) %collective-permute-start.11) | collective-permute-done | bytes 131104 | tf_op jit(solution)/shard_map/ppermute | solution.py:269
  54.6 0.7 %collective-permute-done.12.refs_1_.refs_10_ = f32[2,4,64,128]{3,2,1,0:T(8,128)S(1)} collective-permute-done((f32[2,4,64,128]{3,2,1,0:T(8,128)S(1)}, f32[2,4,64,128]{3,2,1,0:T(8,128)S(1)}, u32[]{:S(2)}, u32[]{:S(2)}) %collective-permute-start.12) | collective-permute-done | bytes 262176 | tf_op jit(solution)/shard_map/ppermute | solution.py:261
  55.4 2.8 %collective-permute-start.13 = (f32[1,4,64,128]{3,2,1,0:T(8,128)S(1)}, f32[1,4,64,128]{3,2,1,0:T(8,128)S(1)}, u32[]{:S(2)}, u32[]{:S(2)}) collective-permute-start(f32[1,4,64,128]{3,2,1,0:T(8,128)S(1)} %summed.7), channel_id=1, source_target_pairs={{0,8},{4,12},{8,0},{12,4},{1,9},{5,13},{9,1},{13,5},{2,10},{6,14},... | collective-permute-start | bytes 393224 | tf_op jit(solution)/shard_map/ppermute | solution.py:269
  58.2 0.1 pad_add_fusion.scalars
  58.2 6.1 %collective-permute-done.13.refs_11_ = f32[1,4,64,128]{3,2,1,0:T(8,128)S(1)} collective-permute-done((f32[1,4,64,128]{3,2,1,0:T(8,128)S(1)}, f32[1,4,64,128]{3,2,1,0:T(8,128)S(1)}, u32[]{:S(2)}, u32[]{:S(2)}) %collective-permute-start.13) | collective-permute-done | bytes 131104 | tf_op jit(solution)/shard_map/ppermute | solution.py:269
  64.3 1.4 %gathered.1 = f32[2,8,64,128]{3,2,1,0:T(8,128)} custom-call(s32[2]{0:T(128)S(1)} %pad_add_fusion.scalars, f32[2,4,64,128]{3,2,1,0:T(8,128)S(1)} %get-tuple-element.15.refs_0_, f32[2,4,64,128]{3,2,1,0:T(8,128)S(1)} %collective-permute-done.2.refs_1_, f32[1,4,64,128]{3,2,1,0:T(8,128)S(1)} %collective-permute-done.3.refs_3_.refs_2_, ...), custom_call_target="tpu_custom_call" | custom-call | tf_op jit(solution)/shard_map/gathered/pallas_call | solution.py:125
  (8 shorter events, 0.1 us)
Async XLA Ops:
  0.0 8.7 %collective-permute-start.1 = (f32[2,8,256,128]{3,2,1,0:T(8,128)}, f32[2,8,256,128]{3,2,1,0:T(8,128)}, u32[]{:S(2)}, u32[]{:S(2)}) collective-permute-start(f32[2,8,256,128]{3,2,1,0:T(8,128)} %refs_2_.7), channel_id=1, source_target_pairs={{0,1},{1,0},{2,3},{3,2},{4,5},{5,4},{6,7},{7,6},{8,9},{9,8},{10,11... | collective-permute-start | bytes 6291464 | tf_op jit(solution)/shard_map/ppermute | solution.py:225
  0.5 8.3 %collective-permute-start = (f32[3,2,128,256]{3,2,1,0:T(8,128)}, f32[3,2,128,256]{3,2,1,0:T(8,128)S(1)}, u32[]{:S(2)}, u32[]{:S(2)}) collective-permute-start(f32[3,2,128,256]{3,2,1,0:T(8,128)} %refs_0_.7), channel_id=1, source_target_pairs={{0,1},{1,0},{2,3},{3,2},{4,5},{5,4},{6,7},{7,6},{8,9},{9,8},{10,11... | collective-permute-start | bytes 2359304 | tf_op jit(solution)/shard_map/ppermute | solution.py:226
  2.0 2.9 %copy-start = (bf16[2,256,2304]{2,1,0:T(8,128)(2,1)}, bf16[2,256,2304]{2,1,0:T(8,128)(2,1)S(1)}, u32[]{:S(2)}) copy-start(bf16[2,256,2304]{2,1,0:T(8,128)(2,1)S(1)} %stage.1.left_cat.earlier) | copy-start | bytes 7077892
  2.1 6.6 %copy-start.3 = (s32[3,2]{0,1:T(2,128)S(1)}, s32[3,2]{0,1:T(2,128)}, u32[]{:S(2)}) copy-start(s32[3,2]{0,1:T(2,128)} %param.7) | copy-start | bytes 76
  4.9 0.8 %copy-start.1 = (f32[4,256,128]{2,1,0:T(8,128)}, f32[4,256,128]{2,1,0:T(8,128)S(1)}, u32[]{:S(2)}) copy-start(f32[4,256,128]{2,1,0:T(8,128)S(1)} %get-tuple-element.22) | copy-start | bytes 1572868
  5.7 15.2 %collective-permute-start.5 = (f32[4,256,128]{2,1,0:T(8,128)}, f32[4,256,128]{2,1,0:T(8,128)S(1)}, u32[]{:S(2)}, u32[]{:S(2)}) collective-permute-start(f32[4,256,128]{2,1,0:T(8,128)} %get-tuple-element.19), channel_id=1, source_target_pairs={{0,2},{2,0},{1,3},{3,1},{4,6},{6,4},{5,7},{7,5},{8,10},{10,8},{9,1... | collective-permute-start | bytes 1572872 | tf_op jit(solution)/shard_map/ppermute | solution.py:241
  12.8 8.0 %collective-permute-start.2 = (f32[2,4,64,128]{3,2,1,0:T(8,128)S(1)}, f32[2,4,64,128]{3,2,1,0:T(8,128)S(1)}, u32[]{:S(2)}, u32[]{:S(2)}) collective-permute-start(f32[2,4,64,128]{3,2,1,0:T(8,128)S(1)} %get-tuple-element.16), channel_id=1, source_target_pairs={{0,4},{4,0},{8,12},{12,8},{1,5},{5,1},{9,13},{13,9},{2,6},{6,2},{1... | collective-permute-start | bytes 786440 | tf_op jit(solution)/shard_map/ppermute | solution.py:261
  18.6 2.4 %copy-start.2 = (f32[4,256,128]{2,1,0:T(8,128)S(1)}, f32[4,256,128]{2,1,0:T(8,128)}, u32[]{:S(2)}) copy-start(f32[4,256,128]{2,1,0:T(8,128)} %copy-done.1) | copy-start | bytes 1572868
  20.9 6.0 %collective-permute-start.6 = (f32[4,256,128]{2,1,0:T(8,128)S(1)}, f32[4,256,128]{2,1,0:T(8,128)S(1)}, u32[]{:S(2)}, u32[]{:S(2)}) collective-permute-start(f32[4,256,128]{2,1,0:T(8,128)S(1)} %relay.2.refs_4_), channel_id=1, source_target_pairs={{0,1},{1,0},{2,3},{3,2},{4,5},{5,4},{6,7},{7,6},{8,9},{9,8},{10,11... | collective-permute-start | bytes 1572872 | tf_op jit(solution)/shard_map/ppermute | solution.py:249
  21.0 14.3 %collective-permute-start.9 = (f32[4,256,128]{2,1,0:T(8,128)S(1)}, f32[4,256,128]{2,1,0:T(8,128)S(1)}, u32[]{:S(2)}, u32[]{:S(2)}) collective-permute-start(f32[4,256,128]{2,1,0:T(8,128)S(1)} %copy-done.2), channel_id=1, source_target_pairs={{0,2},{2,0},{1,3},{3,1},{4,6},{6,4},{5,7},{7,5},{8,10},{10,8},{9,1... | collective-permute-start | bytes 1572872 | tf_op jit(solution)/shard_map/ppermute | solution.py:241
  22.7 11.2 %collective-permute-start.4 = (f32[2,4,64,128]{3,2,1,0:T(8,128)S(1)}, f32[2,4,64,128]{3,2,1,0:T(8,128)S(1)}, u32[]{:S(2)}, u32[]{:S(2)}) collective-permute-start(f32[2,4,64,128]{3,2,1,0:T(8,128)S(1)} %get-tuple-element.17.refs_2_), channel_id=1, source_target_pairs={{0,4},{4,0},{8,12},{12,8},{1,5},{5,1},{9,13},{13,9},{2,6},{6,2},{1... | collective-permute-start | bytes 786440 | tf_op jit(solution)/shard_map/ppermute | solution.py:261
  24.3 9.7 %collective-permute-start.3 = (f32[1,4,64,128]{3,2,1,0:T(8,128)S(1)}, f32[1,4,64,128]{3,2,1,0:T(8,128)S(1)}, u32[]{:S(2)}, u32[]{:S(2)}) collective-permute-start(f32[1,4,64,128]{3,2,1,0:T(8,128)S(1)} %summed.4.earlier.refs_6_), channel_id=1, source_target_pairs={{0,8},{4,12},{8,0},{12,4},{1,9},{5,13},{9,1},{13,5},{2,10},{6,14},... | collective-permute-start | bytes 393224 | tf_op jit(solution)/shard_map/ppermute | solution.py:269
  35.3 4.4 %collective-permute-start.10 = (f32[4,256,128]{2,1,0:T(8,128)S(1)}, f32[4,256,128]{2,1,0:T(8,128)S(1)}, u32[]{:S(2)}, u32[]{:S(2)}) collective-permute-start(f32[4,256,128]{2,1,0:T(8,128)S(1)} %relay.3.refs_4_), channel_id=1, source_target_pairs={{0,1},{1,0},{2,3},{3,2},{4,5},{5,4},{6,7},{7,6},{8,9},{9,8},{10,11... | collective-permute-start | bytes 1572872 | tf_op jit(solution)/shard_map/ppermute | solution.py:249
  35.3 11.8 %collective-permute-start.8 = (f32[2,4,64,128]{3,2,1,0:T(8,128)S(1)}, f32[2,4,64,128]{3,2,1,0:T(8,128)S(1)}, u32[]{:S(2)}, u32[]{:S(2)}) collective-permute-start(f32[2,4,64,128]{3,2,1,0:T(8,128)S(1)} %get-tuple-element.20.refs_2_), channel_id=1, source_target_pairs={{0,4},{4,0},{8,12},{12,8},{1,5},{5,1},{9,13},{13,9},{2,6},{6,2},{1... | collective-permute-start | bytes 786440 | tf_op jit(solution)/shard_map/ppermute | solution.py:261
  37.1 9.4 %collective-permute-start.7 = (f32[1,4,64,128]{3,2,1,0:T(8,128)S(1)}, f32[1,4,64,128]{3,2,1,0:T(8,128)S(1)}, u32[]{:S(2)}, u32[]{:S(2)}) collective-permute-start(f32[1,4,64,128]{3,2,1,0:T(8,128)S(1)} %summed.5.earlier.refs_6_), channel_id=1, source_target_pairs={{0,8},{4,12},{8,0},{12,4},{1,9},{5,13},{9,1},{13,5},{2,10},{6,14},... | collective-permute-start | bytes 393224 | tf_op jit(solution)/shard_map/ppermute | solution.py:269
  44.0 11.3 %collective-permute-start.12 = (f32[2,4,64,128]{3,2,1,0:T(8,128)S(1)}, f32[2,4,64,128]{3,2,1,0:T(8,128)S(1)}, u32[]{:S(2)}, u32[]{:S(2)}) collective-permute-start(f32[2,4,64,128]{3,2,1,0:T(8,128)S(1)} %get-tuple-element.23.refs_2_), channel_id=1, source_target_pairs={{0,4},{4,0},{8,12},{12,8},{1,5},{5,1},{9,13},{13,9},{2,6},{6,2},{1... | collective-permute-start | bytes 786440 | tf_op jit(solution)/shard_map/ppermute | solution.py:261
  47.2 7.5 %collective-permute-start.11 = (f32[1,4,64,128]{3,2,1,0:T(8,128)S(1)}, f32[1,4,64,128]{3,2,1,0:T(8,128)S(1)}, u32[]{:S(2)}, u32[]{:S(2)}) collective-permute-start(f32[1,4,64,128]{3,2,1,0:T(8,128)S(1)} %summed.6), channel_id=1, source_target_pairs={{0,8},{4,12},{8,0},{12,4},{1,9},{5,13},{9,1},{13,5},{2,10},{6,14},... | collective-permute-start | bytes 393224 | tf_op jit(solution)/shard_map/ppermute | solution.py:269
  55.4 9.0 %collective-permute-start.13 = (f32[1,4,64,128]{3,2,1,0:T(8,128)S(1)}, f32[1,4,64,128]{3,2,1,0:T(8,128)S(1)}, u32[]{:S(2)}, u32[]{:S(2)}) collective-permute-start(f32[1,4,64,128]{3,2,1,0:T(8,128)S(1)} %summed.7), channel_id=1, source_target_pairs={{0,8},{4,12},{8,0},{12,4},{1,9},{5,13},{9,1},{13,5},{2,10},{6,14},... | collective-permute-start | bytes 393224 | tf_op jit(solution)/shard_map/ppermute | solution.py:269

commit v3 on v2

--- a/solution.py
+++ b/solution.py
@@ -27,48 +27,46 @@
     return [pltpu.with_memory_space_constraint(value, space) for value in values]
 
 
-def edge_kernel(count, scalars, psi, earlier, *refs):
-    edges, sem = refs[:-1], refs[-1]
-    copies = [
-        pltpu.make_async_copy(psi.at[scalars[0], pl.ds(c * count, count)], edge, sem.at[c]) for c, edge in enumerate(edges)
-    ]
+def edge_kernel(first, scalars, psi, *refs):
+    edge, sem = refs[-2:]
+    copies = [pltpu.make_async_copy(psi.at[scalars[0], first + v], edge.at[v], sem.at[v]) for v in range(edge.shape[0])]
     for copy in copies:
         copy.start()
     for copy in copies:
         copy.wait()
 
 
-def edges_of(sector, psi, count, earlier):
-    chunks = psi.shape[1] // count
-    edge = jax.ShapeDtypeStruct((count,) + psi.shape[2:], psi.dtype)
-    return pl.pallas_call(
-        functools.partial(edge_kernel, count),
-        out_shape=[edge] * chunks,
-        in_specs=[pl.BlockSpec(memory_space=pltpu.SMEM), pl.BlockSpec(memory_space=pltpu.HBM), ANY],
-        out_specs=[VMEM] * chunks,
-        scratch_shapes=[pltpu.SemaphoreType.DMA((chunks,))],
+def edge_of(sector, psi, first, count, *earlier):
+    return pl.pallas_call(
+        functools.partial(edge_kernel, first),
+        out_shape=jax.ShapeDtypeStruct((count,) + psi.shape[2:], psi.dtype),
+        in_specs=[pl.BlockSpec(memory_space=pltpu.SMEM), pl.BlockSpec(memory_space=pltpu.HBM)] + [ANY] * len(earlier),
+        out_specs=VMEM,
+        scratch_shapes=[pltpu.SemaphoreType.DMA((count,))],
         compiler_params=pltpu.CompilerParams(vmem_limit_bytes=1024 * 1024),
-        name="edges",
-    )(jnp.reshape(sector, (1,)), *pinned(pltpu.HBM, psi), earlier)
-
-
-def relay_kernel(value, earlier, out):
+        cost_estimate=pl.CostEstimate(flops=1024, bytes_accessed=1024, transcendentals=0),
+        name="edge",
+    )(jnp.reshape(sector, (1,)), *pinned(pltpu.HBM, psi), *earlier)
+
+
+def relay_kernel(*refs):
     pass
 
 
-def relay(value, earlier):
+def relay(value, *earlier):
     return pl.pallas_call(
         relay_kernel,
         out_shape=jax.ShapeDtypeStruct(value.shape, value.dtype),
-        in_specs=[ANY, ANY],
+        in_specs=[ANY] * (1 + len(earlier)),
         out_specs=ANY,
         input_output_aliases={0: 0},
         compiler_params=pltpu.CompilerParams(vmem_limit_bytes=1024 * 1024),
+        cost_estimate=pl.CostEstimate(flops=1024, bytes_accessed=1024, transcendentals=0),
         name="relay",
-    )(value, earlier)
-
-
-def stage_kernel(order, scalars, left, left_cat):
+    )(value, *earlier)
+
+
+def stage_kernel(order, scalars, left, earlier, left_cat):
     terms, rows, depth = left.shape[0], left.shape[2], left.shape[3]
     piece = rows // len(order)
     for t in range(terms):
@@ -80,7 +78,7 @@
         left_cat[0, :, start + 2 * depth:start + 3 * depth] = low
 
 
-def staged(place, left, order):
+def staged(place, left, order, earlier):
     terms, sectors, rows, depth = left.shape
     return pl.pallas_call(
         functools.partial(stage_kernel, order),
@@ -88,12 +86,13 @@
         grid_spec=pltpu.PrefetchScalarGridSpec(
             num_scalar_prefetch=1,
             grid=(sectors,),
-            in_specs=[pl.BlockSpec((terms, 1, rows, depth), lambda i, s: (0, i, 0, 0))],
+            in_specs=[pl.BlockSpec((terms, 1, rows, depth), lambda i, s: (0, i, 0, 0)), ANY],
             out_specs=pl.BlockSpec((1, rows, terms * 3 * depth), lambda i, s: (i, 0, 0)),
         ),
         compiler_params=pltpu.CompilerParams(vmem_limit_bytes=16 * 1024 * 1024),
+        cost_estimate=pl.CostEstimate(flops=1024, bytes_accessed=1024, transcendentals=0),
         name="stage",
-    )(jnp.reshape(place, (1,)), *pinned(pltpu.HBM, left))
+    )(jnp.reshape(place, (1,)), *pinned(pltpu.HBM, left), earlier)
 
 
 def summed(addends, size, earlier):
@@ -107,13 +106,14 @@
         in_specs=[VMEM] * len(addends) + [ANY] * len(earlier),
         out_specs=VMEM,
         compiler_params=pltpu.CompilerParams(vmem_limit_bytes=4 * 1024 * 1024),
+        cost_estimate=pl.CostEstimate(flops=1024, bytes_accessed=1024, transcendentals=0),
         name="summed",
     )(*[array for array, start in addends], *earlier)
 
 
 def gather_kernel(counts, scalars, *refs):
     out, at = refs[-1], 0
-    for which, first, starts in counts:
+    for (which, first, _), starts in counts:
         total = functools.reduce(lambda a, b: a + b, [ref[start] for ref, start in zip(refs[at:], starts)])
         out[scalars[which], first:first + total.shape[0]] = total
         at += len(starts)
@@ -123,32 +123,42 @@
     addends = [addend for item in items.values() for addend in item]
 
     return pl.pallas_call(
-        functools.partial(gather_kernel, [(*item, [start for array, start in each]) for item, each in items.items()]),
+        functools.partial(gather_kernel, [(item, [start for array, start in each]) for item, each in items.items()]),
         out_shape=jax.ShapeDtypeStruct(shape, jnp.float32),
         in_specs=[pl.BlockSpec(memory_space=pltpu.SMEM)] + [VMEM] * len(addends),
         out_specs=VMEM,
         compiler_params=pltpu.CompilerParams(vmem_limit_bytes=8 * 1024 * 1024),
+        cost_estimate=pl.CostEstimate(flops=1024, bytes_accessed=1024, transcendentals=0),
         name="gathered",
     )(jnp.stack(targets), *[array for array, start in addends])
 
 
 def chunk_kernel(order, terms, first, count, with_halo, scalars, left_cat, *refs):
-    rights, psis, halos = refs[:2], refs[2:4], refs[4:4 + 2 * with_halo]
+    rights, psis, halos = refs[:2], refs[2:4], refs[4:4 + with_halo]
     sent, kept, left_in, right_in, psi_in, right_cat, psi_cat, mid_cat, sem = refs[-9:]
     depth, width = psis[0].shape[2:]
     columns = right_in.shape[3]
     piece = left_in.shape[0] // len(order)
-    sources = 2 + with_halo
+    sources = 2 + (with_halo > 0)
     target, here = scalars[0], pl.ds(pl.multiple_of(scalars[1] * columns, columns), columns)
 
     right_copies = [pltpu.make_async_copy(rights[at].at[:, target, :, here], right_in.at[at], sem.at[at]) for at in range(2)]
     psi_copies = {}
     for source in range(sources):
         for at in range(2):
-            origin = psis[at].at[source, pl.ds(first, count)] if source < 2 else halos[at]
-            psi_copies[source, at] = pltpu.make_async_copy(origin, psi_in.at[source, at], sem.at[2 + 2 * source + at])
-    left_copy = pltpu.make_async_copy(left_cat.at[target], left_in, sem.at[2 + 2 * sources])
-    for copy in right_copies + list(psi_copies.values()) + [left_copy]:
+            place = psi_in.at[source, at]
+            if source < 2:
+                copies = [(psis[at].at[source, pl.ds(first, count)], place)]
+            elif at == 0:
+                copies = [(halos[0], place)]
+            else:
+                size = count // (with_halo - 1)
+                copies = [(ref, place.at[pl.ds(v * size, size)]) for v, ref in enumerate(halos[1:])]
+            psi_copies[source, at] = [
+                pltpu.make_async_copy(*copy, sem.at[3 + 2 * source + at + v]) for v, copy in enumerate(copies)
+            ]
+    left_copy = pltpu.make_async_copy(left_cat.at[target], left_in, sem.at[2])
+    for copy in right_copies + sum(psi_copies.values(), []) + [left_copy]:
         copy.start()
 
     for at in range(2):
@@ -160,7 +170,8 @@
                 right_cat[t, again:again + width, columns:2 * columns] = low
     for source in range(sources):
         for at in range(2):
-            psi_copies[source, at].wait()
+            for copy in psi_copies[source, at]:
+                copy.wait()
             for v in range(count):
                 high, low = halves(psi_in[source, at, v])
                 psi_cat[source, v * depth:(v + 1) * depth, at * width:(at + 1) * width] = high
@@ -186,11 +197,11 @@
     rows = left_cat.shape[1]
     depth, width = psis[0].shape[2:]
     terms, columns = rights[0].shape[0], rights[0].shape[3] // 2
-    with_halo = halos is not None
+    with_halo = len(halos or ())
     args = pinned(pltpu.HBM, left_cat, rights[0]) + [rights[1]] + pinned(pltpu.HBM, psis[0]) + [psis[1], *(halos or ()), *earlier]
     out = jax.ShapeDtypeStruct((len(order) // 2, count, rows // len(order), columns), jnp.float32)
     flops = 2 * 3 * terms * count * rows * columns * (depth + 2 * width)
-    sources = 2 + with_halo
+    sources = 2 + (with_halo > 0)
     return pl.pallas_call(
         functools.partial(chunk_kernel, order, terms, first, count, with_halo),
         out_shape=(out, out),
@@ -203,10 +214,10 @@
             pltpu.VMEM((terms, 4 * width, 2 * columns), jnp.bfloat16),
             pltpu.VMEM((sources, count * depth, 4 * width), jnp.bfloat16),
             pltpu.VMEM((terms * 3 * depth, count * columns), jnp.bfloat16),
-            pltpu.SemaphoreType.DMA((3 + 2 * sources,)),
+            pltpu.SemaphoreType.DMA((3 + 2 * sources + with_halo,)),
         ],
         compiler_params=pltpu.CompilerParams(vmem_limit_bytes=20 * 1024 * 1024),
-        cost_estimate=pl.CostEstimate(flops=flops, bytes_accessed=8 * 1024 * 1024, transcendentals=0),
+        cost_estimate=pl.CostEstimate(flops=1024, bytes_accessed=1024, transcendentals=0),
         name="terms_of_sector",
     )(scalars, *args)
 
@@ -224,7 +235,7 @@
     count = vectors // CHUNKS
     psis = [wavefunction, lax.ppermute(wavefunction, "sub", swap)]
     rights = [right_operators, lax.ppermute(right_operators, "sub", swap)]
-    left_cat = staged(z, left_operators, order)
+    left_cat = None
 
     targets = (x, 1 - x) if places == 2 else (jnp.int32(0), jnp.int32(1))
 
@@ -236,37 +247,52 @@
     halos = {}
     for which in range(2):
         if ways[which] is not None:
-            edges = edges_of(ways[which][0], wavefunction, count, left_cat)
-            for c, edge in enumerate(edges):
-                halos[which, c * count] = lax.ppermute(edge, "sec", ways[which][1])
-
-    def compute(item, earlier):
-        which, first = item
+            for first in range(0, vectors, count):
+                edge = edge_of(ways[which][0], wavefunction, first, count, *([] if left_cat is None else [left_cat]))
+                halos[which, first] = lax.ppermute(edge, "sec", ways[which][1])
+                if left_cat is None:
+                    left_cat = staged(z, left_operators, order, edge)
+
+    def compute(item, earlier, tie):
+        which, first, count = item
         sources = lax.dynamic_index_in_dim(picks, targets[which], 1, keepdims=False)
         both = None
-        if item in halos:
-            halo = halos[item] if earlier is None else relay(halos[item], earlier)
-            both = [halo, lax.ppermute(halo, "sub", swap)]
+        if (which, first) in halos:
+            halo = relay(halos[which, first], *tie) if tie is not None else halos[which, first]
+            both = [halo] + [lax.ppermute(halo[v:v + 1], "sub", swap) for v in range(0, count, 1)]
         else:
             sources = jnp.minimum(sources, 1)
         scalars = jnp.concatenate([jnp.stack([targets[which], core]), sources])
-        return chunk(scalars, left_cat, rights, psis, both, first, count, order, [] if earlier is None else [earlier])
-
-    work = [(which, first) for which in range(2) for first in range(0, vectors, count)]
-    parts, last, newest = {}, None, None
-    for at in range(len(work) + len(stages) - 1):
-        if at < len(work):
-            item = work[at]
-            newest, kept = compute(item, last)
-            parts[item] = [(kept, 0), (lax.ppermute(newest, "term", stages[0]), 0)]
-        for stage in range(1, len(stages)):
-            if 0 <= at - stage < len(work):
-                item = work[at - stage]
-                half = peers >> (stage + 1)
-                behind = parts[work[at - stage - 1]][-1:] if at > stage else []
-                last = summed(parts[item], half, [newest] + [array for array, start in behind])
-                parts[item] = [(array, start + half) for array, start in parts[item]]
-                parts[item].append((lax.ppermute(last, "term", stages[stage]), 0))
+        return chunk(scalars, left_cat, rights, psis, both, first, count, order, earlier)
+
+    work = [(which, first, count) for which in range(2) for first in range(0, vectors, count)]
+    parts = {}
+
+    def begin(item, earlier=(), tie=None):
+        sent, kept = compute(item, list(earlier), tie)
+        parts[item] = [(kept, 0), (lax.ppermute(sent, "term", stages[0]), 0)]
+        return sent
+
+    def proceed(item, stage, earlier=()):
+        half = peers >> (stage + 1)
+        sent = summed(parts[item], half, list(earlier))
+        parts[item] = [(array, start + half) for array, start in parts[item]]
+        parts[item].append((lax.ppermute(sent, "term", stages[stage]), 0))
+        return sent
+
+    late = range(1, len(stages))
+    a1, a2, b1, b2 = work
+    sent = begin(a1)
+    sent = begin(a2)
+    first = sent
+    last = [proceed(a1, stage, [sent]) for stage in late][-1]
+    sent = begin(b1, tie=[last])
+    last = [proceed(a2, stage, [sent]) for stage in late][-1]
+    sent = begin(b2, [parts[a1][-1][0]], tie=[last])
+    for stage in late:
+        proceed(b1, stage, [sent])
+    for stage in late:
+        proceed(b2, stage)
     return gathered(targets, parts, (sectors, vectors) + parts[work[0]][0][0].shape[2:])
 
 

time: 66 us -> 62.8 us (0.952)
  starting transfers between devices: 21.6 us -> 18.5 us
  local copies, waits for them, and re-layouts: 0.8 us -> 1.5 us
    ppermute x12 -> x18, starting transfers between devices: 21.1 us -> 18 us  [the longest x4 7.19 us: proceed(): parts[item].append((lax.ppermute(sent, 'term', stages[stage]), 0))]
    unnamed x8 -> x6, local copies, waits for them, and re-layouts: 0.8 us -> 1.43 us
    ppermute x12 -> x18, waiting for transfers between devices: 20.4 us -> 19.9 us  [the longest x4 11.4 us: begin(): parts[item] = [(kept, 0), (lax.ppermute(sent, 'term', stages[0]), 0)]]
    pallas_call x2 -> x3, Pallas kernels: 4.24 us -> 4.46 us  [the longest x2 3.05 us: edge_of(): pl.pallas_call(functools.partial(edge_kernel, first), out_shape=jax.Shape...]
  transfers between devices with their start and end apart: 14 -> 20, of which waited for: 9 -> 6; matrix products, arithmetic and copies ran while one was open for 0% -> 1% of each run, Pallas kernels for 32% -> 33%
where the time goes in v3:
time: 62.8 us; the launch traced here: 62.5 us
  Pallas kernels  22.2 us (35%)
  waiting for transfers between devices  19.9 us (32%)
  starting transfers between devices  18.5 us (29%)
  local copies, waits for them, and re-layouts  1.5 us (2%)
    pallas_call x4, Pallas kernels, chunk(): pl.pallas_call(functools.partial(chunk_kernel, order, terms, first, count...  16.1 us
    ppermute x4, waiting for transfers between devices, begin(): parts[item] = [(kept, 0), (lax.ppermute(sent, 'term', stages[0]), 0)]  11.4 us
    ppermute x4, waiting for transfers between devices, proceed(): parts[item].append((lax.ppermute(sent, 'term', stages[stage]), 0))  7.96 us
    ppermute x4, starting transfers between devices, proceed(): parts[item].append((lax.ppermute(sent, 'term', stages[stage]), 0))  7.19 us
    ppermute x4, starting transfers between devices, begin(): parts[item] = [(kept, 0), (lax.ppermute(sent, 'term', stages[0]), 0)]  5.38 us
    ppermute x2, starting transfers between devices, shards(): halos[which, first] = lax.ppermute(edge, 'sec', ways[which][1])  3.6 us
    pallas_call x2, Pallas kernels, edge_of(): pl.pallas_call(functools.partial(edge_kernel, first), out_shape=jax.Shape...  3.05 us
    ppermute x8, starting transfers between devices, compute(): lax.ppermute(halo[v:v + 1], 'sub', swap)  1.83 us
  transfers between devices with their start and end apart: 20, of which 6 were waited for; matrix products, arithmetic and copies ran while one was open for 1% of the time, Pallas kernels for 33%

profile of v3, /device:TPU:0, one launch (start us, length us, event | category | flops | bytes accessed | tf_op | source)
XLA Modules:
  0.0 62.5 jit_solution(8593763201600686817)
XLA Ops:
  0.0 0.0 copy-start.2
  0.0 0.5 collective-permute-start.1
  0.5 0.1 collective-permute-start
  0.5 1.9 %edge.2.earlier = f32[4,256,128]{2,1,0:T(8,128)} custom-call(s32[1]{0:T(128)} %bitcast.1.scalars, f32[2,8,256,128]{3,2,1,0:T(8,128)} %refs_2_.7), custom_call_target="tpu_custom_call" | custom-call | flops 1024 | bytes 1024 | tf_op jit(solution)/shard_map/edge/pallas_call | solution.py:40
  2.4 3.0 %collective-permute-start.5 = (f32[4,256,128]{2,1,0:T(8,128)}, f32[4,256,128]{2,1,0:T(8,128)S(1)}, u32[]{:S(2)}, u32[]{:S(2)}) collective-permute-start(f32[4,256,128]{2,1,0:T(8,128)} %edge.2.earlier), channel_id=1, source_target_pairs={{0,2},{2,0},{1,3},{3,1},{4,6},{6,4},{5,7},{7,5},{8,10},{10,8},{9,1... | collective-permute-start | bytes 1572872 | tf_op jit(solution)/shard_map/ppermute | solution.py:252
  5.4 0.0 copy-done.2
  5.5 1.5 %stage.1.left_cat.refs_0_ = bf16[2,256,2304]{2,1,0:T(8,128)(2,1)S(1)} custom-call(s32[1]{0:T(128)} %bitcast.4.scalars, f32[3,2,256,256]{3,2,1,0:T(8,128)} %left.1, f32[4,256,128]{2,1,0:T(8,128)} %edge.2.earlier), custom_call_target="tpu_custom_call" | custom-call | flops 1024 | bytes 1024 | tf_op jit(solution)/shard_map/stage/pallas_call | solution.py:83
  7.0 0.0 copy-start
  7.0 1.4 %copy-done = bf16[2,256,2304]{2,1,0:T(8,128)(2,1)} copy-done((bf16[2,256,2304]{2,1,0:T(8,128)(2,1)}, bf16[2,256,2304]{2,1,0:T(8,128)(2,1)S(1)}, u32[]{:S(2)}) %copy-start) | copy-done | bytes 2359320
  8.4 0.1 pad_add_fusion.1.scalars
  8.5 0.0 copy-start.1
  8.5 0.0 collective-permute-done.refs_1_
  8.5 0.0 collective-permute-done.1.refs_3_
  8.5 4.0 %terms_of_sector.4 = (f32[2,4,64,128]{3,2,1,0:T(8,128)S(1)}, f32[2,4,64,128]{3,2,1,0:T(8,128)S(1)}) custom-call(s32[5]{0:T(128)S(1)} %pad_add_fusion.1.scalars, bf16[2,256,2304]{2,1,0:T(8,128)(2,1)} %copy-done, f32[3,2,128,256]{3,2,1,0:T(8,128)} %refs_0_.7, f32[3,2,128,256]{3,2,1,0:T(8,128)S(1)} %collective-permute-done.refs_1_, f32[2,8,256,128]{3,2,1,0:T(8,128)} %refs_2_.7, ...), custom_call_target="tpu_custom_call" | custom-call | flops 1024 | bytes 1024 | tf_op jit(solution)/shard_map/terms_of_sector/pallas_call | solution.py:205
  12.5 1.6 %collective-permute-start.2 = (f32[2,4,64,128]{3,2,1,0:T(8,128)S(1)}, f32[2,4,64,128]{3,2,1,0:T(8,128)S(1)}, u32[]{:S(2)}, u32[]{:S(2)}) collective-permute-start(f32[2,4,64,128]{3,2,1,0:T(8,128)S(1)} %get-tuple-element.14), channel_id=1, source_target_pairs={{0,4},{4,0},{8,12},{12,8},{1,5},{5,1},{9,13},{13,9},{2,6},{6,2},{1... | collective-permute-start | bytes 786440 | tf_op jit(solution)/shard_map/ppermute | solution.py:273
  14.2 0.0 copy-done.1
  14.2 1.1 %edge.3 = f32[4,256,128]{2,1,0:T(8,128)S(1)} custom-call(s32[1]{0:T(128)} %bitcast.1.scalars, f32[2,8,256,128]{3,2,1,0:T(8,128)} %refs_2_.7, bf16[2,256,2304]{2,1,0:T(8,128)(2,1)S(1)} %copy-done.1), custom_call_target="tpu_custom_call" | custom-call | flops 1024 | bytes 1024 | tf_op jit(solution)/shard_map/edge/pallas_call | solution.py:40
  15.3 0.6 collective-permute-start.12
  15.9 3.9 %terms_of_sector.5 = (f32[2,4,64,128]{3,2,1,0:T(8,128)S(1)}, f32[2,4,64,128]{3,2,1,0:T(8,128)S(1)}) custom-call(s32[5]{0:T(128)S(1)} %pad_add_fusion.1.scalars, bf16[2,256,2304]{2,1,0:T(8,128)(2,1)} %copy-done, f32[3,2,128,256]{3,2,1,0:T(8,128)} %refs_0_.7, f32[3,2,128,256]{3,2,1,0:T(8,128)S(1)} %collective-permute-done.refs_1_, f32[2,8,256,128]{3,2,1,0:T(8,128)} %refs_2_.7, ...), custom_call_target="tpu_custom_call" | custom-call | flops 1024 | bytes 1024 | tf_op jit(solution)/shard_map/terms_of_sector/pallas_call | solution.py:205
  19.8 0.8 %collective-permute-done.2.refs_1_ = f32[2,4,64,128]{3,2,1,0:T(8,128)S(1)} collective-permute-done((f32[2,4,64,128]{3,2,1,0:T(8,128)S(1)}, f32[2,4,64,128]{3,2,1,0:T(8,128)S(1)}, u32[]{:S(2)}, u32[]{:S(2)}) %collective-permute-start.2) | collective-permute-done | bytes 262176 | tf_op jit(solution)/shard_map/ppermute | solution.py:273
  20.6 0.0 collective-permute-done.5.refs_0_
  20.7 0.1 collective-permute-start.9
  20.8 1.6 %collective-permute-start.4 = (f32[2,4,64,128]{3,2,1,0:T(8,128)S(1)}, f32[2,4,64,128]{3,2,1,0:T(8,128)S(1)}, u32[]{:S(2)}, u32[]{:S(2)}) collective-permute-start(f32[2,4,64,128]{3,2,1,0:T(8,128)S(1)} %get-tuple-element.15.refs_2_), channel_id=1, source_target_pairs={{0,4},{4,0},{8,12},{12,8},{1,5},{5,1},{9,13},{13,9},{2,6},{6,2},{1... | collective-permute-start | bytes 786440 | tf_op jit(solution)/shard_map/ppermute | solution.py:273
  22.4 0.2 collective-permute-start.8
  22.6 0.3 collective-permute-start.7
  22.9 0.0 collective-permute-done.9.refs_8_
  22.9 0.2 collective-permute-start.6
  23.1 0.1 pad_add_fusion.2.scalars
  23.2 0.6 collective-permute-done.8.refs_7_
  23.8 2.6 %collective-permute-start.3 = (f32[1,4,64,128]{3,2,1,0:T(8,128)S(1)}, f32[1,4,64,128]{3,2,1,0:T(8,128)S(1)}, u32[]{:S(2)}, u32[]{:S(2)}) collective-permute-start(f32[1,4,64,128]{3,2,1,0:T(8,128)S(1)} %summed.4.refs_1_), channel_id=1, source_target_pairs={{0,8},{4,12},{8,0},{12,4},{1,9},{5,13},{9,1},{13,5},{2,10},{6,14},... | collective-permute-start | bytes 393224 | tf_op jit(solution)/shard_map/ppermute | solution.py:280
  26.3 0.0 collective-permute-done.7.refs_6_
  26.4 0.0 collective-permute-done.6.refs_5_
  26.4 4.1 %terms_of_sector.6 = (f32[2,4,64,128]{3,2,1,0:T(8,128)S(1)}, f32[2,4,64,128]{3,2,1,0:T(8,128)S(1)}) custom-call(s32[5]{0:T(128)S(1)} %pad_add_fusion.2.scalars, bf16[2,256,2304]{2,1,0:T(8,128)(2,1)} %copy-done, f32[3,2,128,256]{3,2,1,0:T(8,128)} %refs_0_.7, f32[3,2,128,256]{3,2,1,0:T(8,128)S(1)} %collective-permute-done.refs_1_, f32[2,8,256,128]{3,2,1,0:T(8,128)} %refs_2_.7, ...), custom_call_target="tpu_custom_call" | custom-call | flops 1024 | bytes 1024 | tf_op jit(solution)/shard_map/terms_of_sector/pallas_call | solution.py:205
  30.5 1.8 %collective-permute-done.4.refs_1_.refs_4_ = f32[2,4,64,128]{3,2,1,0:T(8,128)S(1)} collective-permute-done((f32[2,4,64,128]{3,2,1,0:T(8,128)S(1)}, f32[2,4,64,128]{3,2,1,0:T(8,128)S(1)}, u32[]{:S(2)}, u32[]{:S(2)}) %collective-permute-start.4) | collective-permute-done | bytes 262176 | tf_op jit(solution)/shard_map/ppermute | solution.py:273
  32.3 0.0 collective-permute-done.12.refs_0_
  32.4 0.1 collective-permute-start.16
  32.5 0.5 collective-permute-start.15
  33.0 0.1 collective-permute-start.14
  33.0 0.4 collective-permute-start.13
  33.5 0.0 collective-permute-done.3.refs_9_.refs_2_
  33.5 1.4 %collective-permute-start.11 = (f32[2,4,64,128]{3,2,1,0:T(8,128)S(1)}, f32[2,4,64,128]{3,2,1,0:T(8,128)S(1)}, u32[]{:S(2)}, u32[]{:S(2)}) collective-permute-start(f32[2,4,64,128]{3,2,1,0:T(8,128)S(1)} %get-tuple-element.17.refs_2_), channel_id=1, source_target_pairs={{0,4},{4,0},{8,12},{12,8},{1,5},{5,1},{9,13},{13,9},{2,6},{6,2},{1... | collective-permute-start | bytes 786440 | tf_op jit(solution)/shard_map/ppermute | solution.py:273
  34.9 0.0 collective-permute-done.16.refs_8_
  34.9 0.0 collective-permute-done.15.refs_7_
  34.9 0.0 collective-permute-done.14.refs_6_
  34.9 0.0 collective-permute-done.13.refs_5_
  34.9 4.1 %terms_of_sector.7 = (f32[2,4,64,128]{3,2,1,0:T(8,128)S(1)}, f32[2,4,64,128]{3,2,1,0:T(8,128)S(1)}) custom-call(s32[5]{0:T(128)S(1)} %pad_add_fusion.2.scalars, bf16[2,256,2304]{2,1,0:T(8,128)(2,1)} %copy-done, f32[3,2,128,256]{3,2,1,0:T(8,128)} %refs_0_.7, f32[3,2,128,256]{3,2,1,0:T(8,128)S(1)} %collective-permute-done.refs_1_, f32[2,8,256,128]{3,2,1,0:T(8,128)} %refs_2_.7, ...), custom_call_target="tpu_custom_call" | custom-call | flops 1024 | bytes 1024 | tf_op jit(solution)/shard_map/terms_of_sector/pallas_call | solution.py:205
  39.0 0.7 %collective-permute-start.18 = (f32[2,4,64,128]{3,2,1,0:T(8,128)S(1)}, f32[2,4,64,128]{3,2,1,0:T(8,128)S(1)}, u32[]{:S(2)}, u32[]{:S(2)}) collective-permute-start(f32[2,4,64,128]{3,2,1,0:T(8,128)S(1)} %get-tuple-element.19.refs_2_), channel_id=1, source_target_pairs={{0,4},{4,0},{8,12},{12,8},{1,5},{5,1},{9,13},{13,9},{2,6},{6,2},{1... | collective-permute-start | bytes 786440 | tf_op jit(solution)/shard_map/ppermute | solution.py:273
  39.7 3.1 %collective-permute-start.10 = (f32[1,4,64,128]{3,2,1,0:T(8,128)S(1)}, f32[1,4,64,128]{3,2,1,0:T(8,128)S(1)}, u32[]{:S(2)}, u32[]{:S(2)}) collective-permute-start(f32[1,4,64,128]{3,2,1,0:T(8,128)S(1)} %summed.5.refs_1_), channel_id=1, source_target_pairs={{0,8},{4,12},{8,0},{12,4},{1,9},{5,13},{9,1},{13,5},{2,10},{6,14},... | collective-permute-start | bytes 393224 | tf_op jit(solution)/shard_map/ppermute | solution.py:280
  42.8 0.0 collective-permute-done.11.refs_1_.refs_7_
  42.9 1.4 %collective-permute-start.17 = (f32[1,4,64,128]{3,2,1,0:T(8,128)S(1)}, f32[1,4,64,128]{3,2,1,0:T(8,128)S(1)}, u32[]{:S(2)}, u32[]{:S(2)}) collective-permute-start(f32[1,4,64,128]{3,2,1,0:T(8,128)S(1)} %summed.6), channel_id=1, source_target_pairs={{0,8},{4,12},{8,0},{12,4},{1,9},{5,13},{9,1},{13,5},{2,10},{6,14},... | collective-permute-start | bytes 393224 | tf_op jit(solution)/shard_map/ppermute | solution.py:280
  44.3 8.7 %collective-permute-done.18.refs_1_.refs_10_ = f32[2,4,64,128]{3,2,1,0:T(8,128)S(1)} collective-permute-done((f32[2,4,64,128]{3,2,1,0:T(8,128)S(1)}, f32[2,4,64,128]{3,2,1,0:T(8,128)S(1)}, u32[]{:S(2)}, u32[]{:S(2)}) %collective-permute-start.18) | collective-permute-done | bytes 262176 | tf_op jit(solution)/shard_map/ppermute | solution.py:273
  53.0 0.1 collective-permute-start.19
  53.1 0.1 pad_add_fusion.scalars
  53.2 0.0 collective-permute-done.10.refs_5_
  53.2 1.8 %collective-permute-done.17.refs_8_ = f32[1,4,64,128]{3,2,1,0:T(8,128)S(1)} collective-permute-done((f32[1,4,64,128]{3,2,1,0:T(8,128)S(1)}, f32[1,4,64,128]{3,2,1,0:T(8,128)S(1)}, u32[]{:S(2)}, u32[]{:S(2)}) %collective-permute-start.17) | collective-permute-done | bytes 131104 | tf_op jit(solution)/shard_map/ppermute | solution.py:280
  55.0 6.1 %collective-permute-done.19.refs_11_ = f32[1,4,64,128]{3,2,1,0:T(8,128)S(1)} collective-permute-done((f32[1,4,64,128]{3,2,1,0:T(8,128)S(1)}, f32[1,4,64,128]{3,2,1,0:T(8,128)S(1)}, u32[]{:S(2)}, u32[]{:S(2)}) %collective-permute-start.19) | collective-permute-done | bytes 131104 | tf_op jit(solution)/shard_map/ppermute | solution.py:280
  61.1 1.4 %gathered.1 = f32[2,8,64,128]{3,2,1,0:T(8,128)} custom-call(s32[2]{0:T(128)S(1)} %pad_add_fusion.scalars, f32[2,4,64,128]{3,2,1,0:T(8,128)S(1)} %get-tuple-element.13.refs_0_, f32[2,4,64,128]{3,2,1,0:T(8,128)S(1)} %collective-permute-done.2.refs_1_, f32[1,4,64,128]{3,2,1,0:T(8,128)S(1)} %collective-permute-done.3.refs_9_.refs_2_, ...), custom_call_target="tpu_custom_call" | custom-call | flops 1024 | bytes 1024 | tf_op jit(solution)/shard_map/gathered/pallas_call | solution.py:125
  (10 shorter events, 0.1 us)
Async XLA Ops:
  0.0 5.4 %copy-start.2 = (s32[3,2]{0,1:T(2,128)S(1)}, s32[3,2]{0,1:T(2,128)}, u32[]{:S(2)}) copy-start(s32[3,2]{0,1:T(2,128)} %param.7) | copy-start | bytes 76
  0.0 8.5 %collective-permute-start.1 = (f32[2,8,256,128]{3,2,1,0:T(8,128)}, f32[2,8,256,128]{3,2,1,0:T(8,128)S(1)}, u32[]{:S(2)}, u32[]{:S(2)}) collective-permute-start(f32[2,8,256,128]{3,2,1,0:T(8,128)} %refs_2_.7), channel_id=1, source_target_pairs={{0,1},{1,0},{2,3},{3,2},{4,5},{5,4},{6,7},{7,6},{8,9},{9,8},{10,11... | collective-permute-start | bytes 6291464 | tf_op jit(solution)/shard_map/ppermute | solution.py:236
  0.5 8.1 %collective-permute-start = (f32[3,2,128,256]{3,2,1,0:T(8,128)}, f32[3,2,128,256]{3,2,1,0:T(8,128)S(1)}, u32[]{:S(2)}, u32[]{:S(2)}) collective-permute-start(f32[3,2,128,256]{3,2,1,0:T(8,128)} %refs_0_.7), channel_id=1, source_target_pairs={{0,1},{1,0},{2,3},{3,2},{4,5},{5,4},{6,7},{7,6},{8,9},{9,8},{10,11... | collective-permute-start | bytes 2359304 | tf_op jit(solution)/shard_map/ppermute | solution.py:237
  2.4 18.2 %collective-permute-start.5 = (f32[4,256,128]{2,1,0:T(8,128)}, f32[4,256,128]{2,1,0:T(8,128)S(1)}, u32[]{:S(2)}, u32[]{:S(2)}) collective-permute-start(f32[4,256,128]{2,1,0:T(8,128)} %edge.2.earlier), channel_id=1, source_target_pairs={{0,2},{2,0},{1,3},{3,1},{4,6},{6,4},{5,7},{7,5},{8,10},{10,8},{9,1... | collective-permute-start | bytes 1572872 | tf_op jit(solution)/shard_map/ppermute | solution.py:252
  7.0 1.4 %copy-start = (bf16[2,256,2304]{2,1,0:T(8,128)(2,1)}, bf16[2,256,2304]{2,1,0:T(8,128)(2,1)S(1)}, u32[]{:S(2)}) copy-start(bf16[2,256,2304]{2,1,0:T(8,128)(2,1)S(1)} %stage.1.left_cat.refs_0_) | copy-start | bytes 7077892
  8.5 5.7 %copy-start.1 = (bf16[2,256,2304]{2,1,0:T(8,128)(2,1)S(1)}, bf16[2,256,2304]{2,1,0:T(8,128)(2,1)}, u32[]{:S(2)}) copy-start(bf16[2,256,2304]{2,1,0:T(8,128)(2,1)} %copy-done) | copy-start | bytes 7077892
  12.5 8.1 %collective-permute-start.2 = (f32[2,4,64,128]{3,2,1,0:T(8,128)S(1)}, f32[2,4,64,128]{3,2,1,0:T(8,128)S(1)}, u32[]{:S(2)}, u32[]{:S(2)}) collective-permute-start(f32[2,4,64,128]{3,2,1,0:T(8,128)S(1)} %get-tuple-element.14), channel_id=1, source_target_pairs={{0,4},{4,0},{8,12},{12,8},{1,5},{5,1},{9,13},{13,9},{2,6},{6,2},{1... | collective-permute-start | bytes 786440 | tf_op jit(solution)/shard_map/ppermute | solution.py:273
  15.3 17.0 %collective-permute-start.12 = (f32[4,256,128]{2,1,0:T(8,128)S(1)}, f32[4,256,128]{2,1,0:T(8,128)S(1)}, u32[]{:S(2)}, u32[]{:S(2)}) collective-permute-start(f32[4,256,128]{2,1,0:T(8,128)S(1)} %edge.3), channel_id=1, source_target_pairs={{0,2},{2,0},{1,3},{3,1},{4,6},{6,4},{5,7},{7,5},{8,10},{10,8},{9,1... | collective-permute-start | bytes 1572872 | tf_op jit(solution)/shard_map/ppermute | solution.py:252
  20.7 2.2 %collective-permute-start.9 = (f32[1,256,128]{2,1,0:T(8,128)S(1)}, f32[1,256,128]{2,1,0:T(8,128)S(1)}, u32[]{:S(2)}, u32[]{:S(2)}) collective-permute-start(f32[1,256,128]{2,1,0:T(8,128)S(1)} %get-tuple-element.25), channel_id=1, source_target_pairs={{0,1},{1,0},{2,3},{3,2},{4,5},{5,4},{6,7},{7,6},{8,9},{9,8},{10,11... | collective-permute-start | bytes 393224 | tf_op jit(solution)/shard_map/ppermute | solution.py:262
  20.8 11.5 %collective-permute-start.4 = (f32[2,4,64,128]{3,2,1,0:T(8,128)S(1)}, f32[2,4,64,128]{3,2,1,0:T(8,128)S(1)}, u32[]{:S(2)}, u32[]{:S(2)}) collective-permute-start(f32[2,4,64,128]{3,2,1,0:T(8,128)S(1)} %get-tuple-element.15.refs_2_), channel_id=1, source_target_pairs={{0,4},{4,0},{8,12},{12,8},{1,5},{5,1},{9,13},{13,9},{2,6},{6,2},{1... | collective-permute-start | bytes 786440 | tf_op jit(solution)/shard_map/ppermute | solution.py:273
  22.4 1.3 %collective-permute-start.8 = (f32[1,256,128]{2,1,0:T(8,128)S(1)}, f32[1,256,128]{2,1,0:T(8,128)S(1)}, u32[]{:S(2)}, u32[]{:S(2)}) collective-permute-start(f32[1,256,128]{2,1,0:T(8,128)S(1)} %get-tuple-element.26), channel_id=1, source_target_pairs={{0,1},{1,0},{2,3},{3,2},{4,5},{5,4},{6,7},{7,6},{8,9},{9,8},{10,11... | collective-permute-start | bytes 393224 | tf_op jit(solution)/shard_map/ppermute | solution.py:262
  22.6 3.8 %collective-permute-start.7 = (f32[1,256,128]{2,1,0:T(8,128)S(1)}, f32[1,256,128]{2,1,0:T(8,128)S(1)}, u32[]{:S(2)}, u32[]{:S(2)}) collective-permute-start(f32[1,256,128]{2,1,0:T(8,128)S(1)} %get-tuple-element.27), channel_id=1, source_target_pairs={{0,1},{1,0},{2,3},{3,2},{4,5},{5,4},{6,7},{7,6},{8,9},{9,8},{10,11... | collective-permute-start | bytes 393224 | tf_op jit(solution)/shard_map/ppermute | solution.py:262
  22.9 3.4 %collective-permute-start.6 = (f32[1,256,128]{2,1,0:T(8,128)S(1)}, f32[1,256,128]{2,1,0:T(8,128)S(1)}, u32[]{:S(2)}, u32[]{:S(2)}) collective-permute-start(f32[1,256,128]{2,1,0:T(8,128)S(1)} %get-tuple-element.28), channel_id=1, source_target_pairs={{0,1},{1,0},{2,3},{3,2},{4,5},{5,4},{6,7},{7,6},{8,9},{9,8},{10,11... | collective-permute-start | bytes 393224 | tf_op jit(solution)/shard_map/ppermute | solution.py:262
  23.8 9.7 %collective-permute-start.3 = (f32[1,4,64,128]{3,2,1,0:T(8,128)S(1)}, f32[1,4,64,128]{3,2,1,0:T(8,128)S(1)}, u32[]{:S(2)}, u32[]{:S(2)}) collective-permute-start(f32[1,4,64,128]{3,2,1,0:T(8,128)S(1)} %summed.4.refs_1_), channel_id=1, source_target_pairs={{0,8},{4,12},{8,0},{12,4},{1,9},{5,13},{9,1},{13,5},{2,10},{6,14},... | collective-permute-start | bytes 393224 | tf_op jit(solution)/shard_map/ppermute | solution.py:280
  32.4 2.5 %collective-permute-start.16 = (f32[1,256,128]{2,1,0:T(8,128)S(1)}, f32[1,256,128]{2,1,0:T(8,128)S(1)}, u32[]{:S(2)}, u32[]{:S(2)}) collective-permute-start(f32[1,256,128]{2,1,0:T(8,128)S(1)} %get-tuple-element.21), channel_id=1, source_target_pairs={{0,1},{1,0},{2,3},{3,2},{4,5},{5,4},{6,7},{7,6},{8,9},{9,8},{10,11... | collective-permute-start | bytes 393224 | tf_op jit(solution)/shard_map/ppermute | solution.py:262
  32.5 2.4 %collective-permute-start.15 = (f32[1,256,128]{2,1,0:T(8,128)S(1)}, f32[1,256,128]{2,1,0:T(8,128)S(1)}, u32[]{:S(2)}, u32[]{:S(2)}) collective-permute-start(f32[1,256,128]{2,1,0:T(8,128)S(1)} %get-tuple-element.22), channel_id=1, source_target_pairs={{0,1},{1,0},{2,3},{3,2},{4,5},{5,4},{6,7},{7,6},{8,9},{9,8},{10,11... | collective-permute-start | bytes 393224 | tf_op jit(solution)/shard_map/ppermute | solution.py:262
  33.0 1.9 %collective-permute-start.14 = (f32[1,256,128]{2,1,0:T(8,128)S(1)}, f32[1,256,128]{2,1,0:T(8,128)S(1)}, u32[]{:S(2)}, u32[]{:S(2)}) collective-permute-start(f32[1,256,128]{2,1,0:T(8,128)S(1)} %get-tuple-element.23), channel_id=1, source_target_pairs={{0,1},{1,0},{2,3},{3,2},{4,5},{5,4},{6,7},{7,6},{8,9},{9,8},{10,11... | collective-permute-start | bytes 393224 | tf_op jit(solution)/shard_map/ppermute | solution.py:262
  33.0 1.9 %collective-permute-start.13 = (f32[1,256,128]{2,1,0:T(8,128)S(1)}, f32[1,256,128]{2,1,0:T(8,128)S(1)}, u32[]{:S(2)}, u32[]{:S(2)}) collective-permute-start(f32[1,256,128]{2,1,0:T(8,128)S(1)} %get-tuple-element.24), channel_id=1, source_target_pairs={{0,1},{1,0},{2,3},{3,2},{4,5},{5,4},{6,7},{7,6},{8,9},{9,8},{10,11... | collective-permute-start | bytes 393224 | tf_op jit(solution)/shard_map/ppermute | solution.py:262
  33.5 9.4 %collective-permute-start.11 = (f32[2,4,64,128]{3,2,1,0:T(8,128)S(1)}, f32[2,4,64,128]{3,2,1,0:T(8,128)S(1)}, u32[]{:S(2)}, u32[]{:S(2)}) collective-permute-start(f32[2,4,64,128]{3,2,1,0:T(8,128)S(1)} %get-tuple-element.17.refs_2_), channel_id=1, source_target_pairs={{0,4},{4,0},{8,12},{12,8},{1,5},{5,1},{9,13},{13,9},{2,6},{6,2},{1... | collective-permute-start | bytes 786440 | tf_op jit(solution)/shard_map/ppermute | solution.py:273
  39.0 14.0 %collective-permute-start.18 = (f32[2,4,64,128]{3,2,1,0:T(8,128)S(1)}, f32[2,4,64,128]{3,2,1,0:T(8,128)S(1)}, u32[]{:S(2)}, u32[]{:S(2)}) collective-permute-start(f32[2,4,64,128]{3,2,1,0:T(8,128)S(1)} %get-tuple-element.19.refs_2_), channel_id=1, source_target_pairs={{0,4},{4,0},{8,12},{12,8},{1,5},{5,1},{9,13},{13,9},{2,6},{6,2},{1... | collective-permute-start | bytes 786440 | tf_op jit(solution)/shard_map/ppermute | solution.py:273
  39.7 13.5 %collective-permute-start.10 = (f32[1,4,64,128]{3,2,1,0:T(8,128)S(1)}, f32[1,4,64,128]{3,2,1,0:T(8,128)S(1)}, u32[]{:S(2)}, u32[]{:S(2)}) collective-permute-start(f32[1,4,64,128]{3,2,1,0:T(8,128)S(1)} %summed.5.refs_1_), channel_id=1, source_target_pairs={{0,8},{4,12},{8,0},{12,4},{1,9},{5,13},{9,1},{13,5},{2,10},{6,14},... | collective-permute-start | bytes 393224 | tf_op jit(solution)/shard_map/ppermute | solution.py:280
  42.9 12.2 %collective-permute-start.17 = (f32[1,4,64,128]{3,2,1,0:T(8,128)S(1)}, f32[1,4,64,128]{3,2,1,0:T(8,128)S(1)}, u32[]{:S(2)}, u32[]{:S(2)}) collective-permute-start(f32[1,4,64,128]{3,2,1,0:T(8,128)S(1)} %summed.6), channel_id=1, source_target_pairs={{0,8},{4,12},{8,0},{12,4},{1,9},{5,13},{9,1},{13,5},{2,10},{6,14},... | collective-permute-start | bytes 393224 | tf_op jit(solution)/shard_map/ppermute | solution.py:280
  53.0 8.1 %collective-permute-start.19 = (f32[1,4,64,128]{3,2,1,0:T(8,128)S(1)}, f32[1,4,64,128]{3,2,1,0:T(8,128)S(1)}, u32[]{:S(2)}, u32[]{:S(2)}) collective-permute-start(f32[1,4,64,128]{3,2,1,0:T(8,128)S(1)} %summed.7), channel_id=1, source_target_pairs={{0,8},{4,12},{8,0},{12,4},{1,9},{5,13},{9,1},{13,5},{2,10},{6,14},... | collective-permute-start | bytes 393224 | tf_op jit(solution)/shard_map/ppermute | solution.py:280

commit v4 on v3

--- a/solution.py
+++ b/solution.py
@@ -7,7 +7,6 @@
 from jax.experimental.pallas import tpu as pltpu
 from jax.sharding import PartitionSpec as P
 
-CHUNKS = 2
 ANY = pl.BlockSpec(memory_space=pl.ANY)
 VMEM = pl.BlockSpec(memory_space=pltpu.VMEM)
 
@@ -198,7 +197,7 @@
     depth, width = psis[0].shape[2:]
     terms, columns = rights[0].shape[0], rights[0].shape[3] // 2
     with_halo = len(halos or ())
-    args = pinned(pltpu.HBM, left_cat, rights[0]) + [rights[1]] + pinned(pltpu.HBM, psis[0]) + [psis[1], *(halos or ()), *earlier]
+    args = [left_cat] + pinned(pltpu.HBM, rights[0]) + [rights[1]] + pinned(pltpu.HBM, psis[0]) + [psis[1], *(halos or ()), *earlier]
     out = jax.ShapeDtypeStruct((len(order) // 2, count, rows // len(order), columns), jnp.float32)
     flops = 2 * 3 * terms * count * rows * columns * (depth + 2 * width)
     sources = 2 + (with_halo > 0)
@@ -232,7 +231,7 @@
     swap = [(0, 1), (1, 0)]
     relative = source_sectors - x * sectors
     picks = jnp.where((relative >= 0) & (relative < sectors), relative, 2)
-    count = vectors // CHUNKS
+    count = vectors // 2
     psis = [wavefunction, lax.ppermute(wavefunction, "sub", swap)]
     rights = [right_operators, lax.ppermute(right_operators, "sub", swap)]
     left_cat = None
@@ -284,7 +283,6 @@
     a1, a2, b1, b2 = work
     sent = begin(a1)
     sent = begin(a2)
-    first = sent
     last = [proceed(a1, stage, [sent]) for stage in late][-1]
     sent = begin(b1, tie=[last])
     last = [proceed(a2, stage, [sent]) for stage in late][-1]
@@ -293,7 +291,9 @@
         proceed(b1, stage, [sent])
     for stage in late:
         proceed(b2, stage)
-    return gathered(targets, parts, (sectors, vectors) + parts[work[0]][0][0].shape[2:])
+    out = gathered(targets, {item: parts[item] for item in (a1, a2, b1)}, (sectors, vectors) + parts[a1][0][0].shape[2:])
+    total = sum(array[start:start + 1] for array, start in parts[b2])
+    return lax.dynamic_update_slice(out, total, (targets[1], b2[1], 0, 0))
 
 
 def solution(mesh):

time: 62.8 us -> 61.9 us (0.986)
  waiting for transfers between devices: 19.9 us -> 17.2 us
  Pallas kernels: 22.2 us -> 22.9 us
  starting transfers between devices: 18.5 us -> 19.2 us
  other arithmetic: 0.24 us -> 0.93 us
    ppermute x4, waiting for transfers between devices: 7.96 us -> 6.2 us  [proceed(): parts[item].append((lax.ppermute(sent, 'term', stages[stage]), 0))]
    unnamed x6 -> x2, local copies, waits for them, and re-layouts: 1.43 us -> 0.01 us
    slice x2, local copies, waits for them, and re-layouts: 0.07 us -> 1.17 us  [compute(): halo[v:v + 1]]
    ppermute x4, waiting for transfers between devices: 11.4 us -> 10.4 us  [begin(): parts[item] = [(kept, 0), (lax.ppermute(sent, 'term', stages[0]), 0)]]
    ppermute x2, starting transfers between devices: 3.6 us -> 4.52 us  [shards(): halos[which, first] = lax.ppermute(edge, 'sec', ways[which][1])]
    pallas_call x4, Pallas kernels: 16.1 us -> 16.9 us  [chunk(): pl.pallas_call(functools.partial(chunk_kernel, order, terms, first, count...]
    dynamic_update_slice x0 -> x1, other arithmetic: none -> 0.68 us  [shards(): return lax.dynamic_update_slice(out, total, (targets[1], b2[1], 0, 0))]
  transfers between devices with their start and end apart: 20 -> 20, of which waited for: 6 -> 4; matrix products, arithmetic and copies ran while one was open for 1% -> 2% of each run, Pallas kernels for 33% -> 37%
where the time goes in v4:
time: 61.9 us; the launch traced here: 61.6 us
  Pallas kernels  22.9 us (37%)
  starting transfers between devices  19.2 us (31%)
  waiting for transfers between devices  17.2 us (28%)
  local copies, waits for them, and re-layouts  1.17 us (2%)
  other arithmetic  0.93 us (2%)
    pallas_call x4, Pallas kernels, chunk(): pl.pallas_call(functools.partial(chunk_kernel, order, terms, first, count...  16.9 us
    ppermute x4, waiting for transfers between devices, begin(): parts[item] = [(kept, 0), (lax.ppermute(sent, 'term', stages[0]), 0)]  10.4 us
    ppermute x4, starting transfers between devices, proceed(): parts[item].append((lax.ppermute(sent, 'term', stages[stage]), 0))  6.97 us
    ppermute x4, waiting for transfers between devices, proceed(): parts[item].append((lax.ppermute(sent, 'term', stages[stage]), 0))  6.2 us
    ppermute x4, starting transfers between devices, begin(): parts[item] = [(kept, 0), (lax.ppermute(sent, 'term', stages[0]), 0)]  5.35 us
    ppermute x2, starting transfers between devices, shards(): halos[which, first] = lax.ppermute(edge, 'sec', ways[which][1])  4.52 us
    pallas_call x2, Pallas kernels, edge_of(): pl.pallas_call(functools.partial(edge_kernel, first), out_shape=jax.Shape...  3.04 us
    ppermute x8, starting transfers between devices, compute(): lax.ppermute(halo[v:v + 1], 'sub', swap)  1.83 us
  transfers between devices with their start and end apart: 20, of which 4 were waited for; matrix products, arithmetic and copies ran while one was open for 2% of the time, Pallas kernels for 37%

profile of v4, /device:TPU:0, one launch (start us, length us, event | category | flops | bytes accessed | tf_op | source)
XLA Modules:
  0.0 61.6 jit_solution(166693006644781181)
XLA Ops:
  0.0 0.0 copy-start
  0.0 0.5 collective-permute-start.1
  0.5 0.1 collective-permute-start
  0.5 1.9 %edge.2.earlier = f32[4,256,128]{2,1,0:T(8,128)} custom-call(s32[1]{0:T(128)} %bitcast.1.scalars, f32[2,8,256,128]{3,2,1,0:T(8,128)} %refs_2_.7), custom_call_target="tpu_custom_call" | custom-call | flops 1024 | bytes 1024 | tf_op jit(solution)/shard_map/edge/pallas_call | solution.py:39
  2.4 3.0 %collective-permute-start.5 = (f32[4,256,128]{2,1,0:T(8,128)}, f32[4,256,128]{2,1,0:T(8,128)}, u32[]{:S(2)}, u32[]{:S(2)}) collective-permute-start(f32[4,256,128]{2,1,0:T(8,128)} %edge.2.earlier), channel_id=1, source_target_pairs={{0,2},{2,0},{1,3},{3,1},{4,6},{6,4},{5,7},{7,5},{8,10},{10,8},{9,1... | collective-permute-start | bytes 1572872 | tf_op jit(solution)/shard_map/ppermute | solution.py:251
  5.4 0.0 copy-done
  5.5 1.5 %stage.1.left_cat.refs_0_ = bf16[2,256,2304]{2,1,0:T(8,128)(2,1)S(1)} custom-call(s32[1]{0:T(128)} %bitcast.4.scalars, f32[3,2,256,256]{3,2,1,0:T(8,128)} %left.1, f32[4,256,128]{2,1,0:T(8,128)} %edge.2.earlier), custom_call_target="tpu_custom_call" | custom-call | flops 1024 | bytes 1024 | tf_op jit(solution)/shard_map/stage/pallas_call | solution.py:82
  7.0 0.1 pad_add_fusion.1.scalars
  7.1 0.0 collective-permute-done.refs_1_
  7.1 0.0 collective-permute-done.1.refs_3_
  7.1 4.1 %terms_of_sector.4 = (f32[2,4,64,128]{3,2,1,0:T(8,128)S(1)}, f32[2,4,64,128]{3,2,1,0:T(8,128)S(1)}) custom-call(s32[5]{0:T(128)S(1)} %pad_add_fusion.1.scalars, bf16[2,256,2304]{2,1,0:T(8,128)(2,1)S(1)} %stage.1.left_cat.refs_0_, f32[3,2,128,256]{3,2,1,0:T(8,128)} %refs_0_.7, f32[3,2,128,256]{3,2,1,0:T(8,128)S(1)} %collective-permute-done.refs_1_, ...), custom_call_target="tpu_custom_call" | custom-call | flops 1024 | bytes 1024 | tf_op jit(solution)/shard_map/terms_of_sector/pallas_call | solution.py:204
  11.2 1.6 %collective-permute-start.2 = (f32[2,4,64,128]{3,2,1,0:T(8,128)S(1)}, f32[2,4,64,128]{3,2,1,0:T(8,128)S(1)}, u32[]{:S(2)}, u32[]{:S(2)}) collective-permute-start(f32[2,4,64,128]{3,2,1,0:T(8,128)S(1)} %get-tuple-element.14), channel_id=1, source_target_pairs={{0,4},{4,0},{8,12},{12,8},{1,5},{5,1},{9,13},{13,9},{2,6},{6,2},{1... | collective-permute-start | bytes 786440 | tf_op jit(solution)/shard_map/ppermute | solution.py:272
  12.8 1.1 %edge.3 = f32[4,256,128]{2,1,0:T(8,128)S(1)} custom-call(s32[1]{0:T(128)} %bitcast.1.scalars, f32[2,8,256,128]{3,2,1,0:T(8,128)} %refs_2_.7, bf16[2,256,2304]{2,1,0:T(8,128)(2,1)S(1)} %stage.1.left_cat.refs_0_), custom_call_target="tpu_custom_call" | custom-call | flops 1024 | bytes 1024 | tf_op jit(solution)/shard_map/edge/pallas_call | solution.py:39
  14.0 1.5 %collective-permute-start.12 = (f32[4,256,128]{2,1,0:T(8,128)S(1)}, f32[4,256,128]{2,1,0:T(8,128)S(1)}, u32[]{:S(2)}, u32[]{:S(2)}) collective-permute-start(f32[4,256,128]{2,1,0:T(8,128)S(1)} %edge.3), channel_id=1, source_target_pairs={{0,2},{2,0},{1,3},{3,1},{4,6},{6,4},{5,7},{7,5},{8,10},{10,8},{9,1... | collective-permute-start | bytes 1572872 | tf_op jit(solution)/shard_map/ppermute | solution.py:251
  15.5 4.1 %terms_of_sector.5 = (f32[2,4,64,128]{3,2,1,0:T(8,128)S(1)}, f32[2,4,64,128]{3,2,1,0:T(8,128)S(1)}) custom-call(s32[5]{0:T(128)S(1)} %pad_add_fusion.1.scalars, bf16[2,256,2304]{2,1,0:T(8,128)(2,1)S(1)} %stage.1.left_cat.refs_0_, f32[3,2,128,256]{3,2,1,0:T(8,128)} %refs_0_.7, f32[3,2,128,256]{3,2,1,0:T(8,128)S(1)} %collective-permute-done.refs_1_, ...), custom_call_target="tpu_custom_call" | custom-call | flops 1024 | bytes 1024 | tf_op jit(solution)/shard_map/terms_of_sector/pallas_call | solution.py:204
  19.6 0.0 collective-permute-done.2.refs_1_
  19.6 0.0 collective-permute-done.5.refs_0_
  19.6 1.1 %fusion.6 = (f32[1,256,128]{2,1,0:T(8,128)S(1)}, f32[1,256,128]{2,1,0:T(8,128)S(1)}, f32[1,256,128]{2,1,0:T(8,128)S(1)}, f32[1,256,128]{2,1,0:T(8,128)S(1)}) fusion(f32[4,256,128]{2,1,0:T(8,128)} %relay.2.refs_4_), kind=kLoop, calls=%fused_computation.13 | loop fusion | bytes 1048576 | tf_op jit(solution)/shard_map/slice | solution.py:261
  20.8 0.1 collective-permute-start.9
  20.8 1.6 %collective-permute-start.4 = (f32[2,4,64,128]{3,2,1,0:T(8,128)S(1)}, f32[2,4,64,128]{3,2,1,0:T(8,128)S(1)}, u32[]{:S(2)}, u32[]{:S(2)}) collective-permute-start(f32[2,4,64,128]{3,2,1,0:T(8,128)S(1)} %get-tuple-element.15.refs_2_), channel_id=1, source_target_pairs={{0,4},{4,0},{8,12},{12,8},{1,5},{5,1},{9,13},{13,9},{2,6},{6,2},{1... | collective-permute-start | bytes 786440 | tf_op jit(solution)/shard_map/ppermute | solution.py:272
  22.5 0.2 collective-permute-start.8
  22.6 0.3 collective-permute-start.7
  23.0 0.0 collective-permute-done.9.refs_8_
  23.0 0.2 collective-permute-start.6
  23.2 0.1 pad_add_fusion.2.scalars
  23.2 0.6 collective-permute-done.8.refs_7_
  23.8 2.6 %collective-permute-start.3 = (f32[1,4,64,128]{3,2,1,0:T(8,128)S(1)}, f32[1,4,64,128]{3,2,1,0:T(8,128)S(1)}, u32[]{:S(2)}, u32[]{:S(2)}) collective-permute-start(f32[1,4,64,128]{3,2,1,0:T(8,128)S(1)} %summed.4.refs_1_), channel_id=1, source_target_pairs={{0,8},{4,12},{8,0},{12,4},{1,9},{5,13},{9,1},{13,5},{2,10},{6,14},... | collective-permute-start | bytes 393224 | tf_op jit(solution)/shard_map/ppermute | solution.py:279
  26.4 0.0 collective-permute-done.7.refs_6_
  26.4 0.0 collective-permute-done.6.refs_5_
  26.4 4.4 %terms_of_sector.6 = (f32[2,4,64,128]{3,2,1,0:T(8,128)S(1)}, f32[2,4,64,128]{3,2,1,0:T(8,128)S(1)}) custom-call(s32[5]{0:T(128)S(1)} %pad_add_fusion.2.scalars, bf16[2,256,2304]{2,1,0:T(8,128)(2,1)S(1)} %stage.1.left_cat.refs_0_, f32[3,2,128,256]{3,2,1,0:T(8,128)} %refs_0_.7, f32[3,2,128,256]{3,2,1,0:T(8,128)S(1)} %collective-permute-done.refs_1_, ...), custom_call_target="tpu_custom_call" | custom-call | flops 1024 | bytes 1024 | tf_op jit(solution)/shard_map/terms_of_sector/pallas_call | solution.py:204
  30.8 1.6 %collective-permute-done.4.refs_1_.refs_4_ = f32[2,4,64,128]{3,2,1,0:T(8,128)S(1)} collective-permute-done((f32[2,4,64,128]{3,2,1,0:T(8,128)S(1)}, f32[2,4,64,128]{3,2,1,0:T(8,128)S(1)}, u32[]{:S(2)}, u32[]{:S(2)}) %collective-permute-start.4) | collective-permute-done | bytes 262176 | tf_op jit(solution)/shard_map/ppermute | solution.py:272
  32.4 0.0 collective-permute-done.12.refs_0_
  32.5 0.1 collective-permute-start.16
  32.5 0.5 collective-permute-start.15
  33.0 0.1 collective-permute-start.14
  33.1 0.4 collective-permute-start.13
  33.6 0.0 collective-permute-done.3.refs_9_.refs_2_
  33.6 1.4 %collective-permute-start.11 = (f32[2,4,64,128]{3,2,1,0:T(8,128)S(1)}, f32[2,4,64,128]{3,2,1,0:T(8,128)S(1)}, u32[]{:S(2)}, u32[]{:S(2)}) collective-permute-start(f32[2,4,64,128]{3,2,1,0:T(8,128)S(1)} %get-tuple-element.17.refs_2_), channel_id=1, source_target_pairs={{0,4},{4,0},{8,12},{12,8},{1,5},{5,1},{9,13},{13,9},{2,6},{6,2},{1... | collective-permute-start | bytes 786440 | tf_op jit(solution)/shard_map/ppermute | solution.py:272
  35.0 0.0 collective-permute-done.16.refs_8_
  35.0 0.0 collective-permute-done.15.refs_7_
  35.0 0.0 collective-permute-done.14.refs_6_
  35.0 0.0 collective-permute-done.13.refs_5_
  35.0 4.3 %terms_of_sector.7 = (f32[2,4,64,128]{3,2,1,0:T(8,128)S(1)}, f32[2,4,64,128]{3,2,1,0:T(8,128)S(1)}) custom-call(s32[5]{0:T(128)S(1)} %pad_add_fusion.2.scalars, bf16[2,256,2304]{2,1,0:T(8,128)(2,1)S(1)} %stage.1.left_cat.refs_0_, f32[3,2,128,256]{3,2,1,0:T(8,128)} %refs_0_.7, f32[3,2,128,256]{3,2,1,0:T(8,128)S(1)} %collective-permute-done.refs_1_, ...), custom_call_target="tpu_custom_call" | custom-call | flops 1024 | bytes 1024 | tf_op jit(solution)/shard_map/terms_of_sector/pallas_call | solution.py:204
  39.3 0.7 %collective-permute-start.18 = (f32[2,4,64,128]{3,2,1,0:T(8,128)S(1)}, f32[2,4,64,128]{3,2,1,0:T(8,128)S(1)}, u32[]{:S(2)}, u32[]{:S(2)}) collective-permute-start(f32[2,4,64,128]{3,2,1,0:T(8,128)S(1)} %get-tuple-element.19.refs_2_), channel_id=1, source_target_pairs={{0,4},{4,0},{8,12},{12,8},{1,5},{5,1},{9,13},{13,9},{2,6},{6,2},{1... | collective-permute-start | bytes 786440 | tf_op jit(solution)/shard_map/ppermute | solution.py:272
  40.0 3.1 %collective-permute-start.10 = (f32[1,4,64,128]{3,2,1,0:T(8,128)S(1)}, f32[1,4,64,128]{3,2,1,0:T(8,128)S(1)}, u32[]{:S(2)}, u32[]{:S(2)}) collective-permute-start(f32[1,4,64,128]{3,2,1,0:T(8,128)S(1)} %summed.5.refs_1_), channel_id=1, source_target_pairs={{0,8},{4,12},{8,0},{12,4},{1,9},{5,13},{9,1},{13,5},{2,10},{6,14},... | collective-permute-start | bytes 393224 | tf_op jit(solution)/shard_map/ppermute | solution.py:279
  43.1 0.0 collective-permute-done.11.refs_1_.refs_7_
  43.1 1.2 %collective-permute-start.17 = (f32[1,4,64,128]{3,2,1,0:T(8,128)S(1)}, f32[1,4,64,128]{3,2,1,0:T(8,128)S(1)}, u32[]{:S(2)}, u32[]{:S(2)}) collective-permute-start(f32[1,4,64,128]{3,2,1,0:T(8,128)S(1)} %summed.6), channel_id=1, source_target_pairs={{0,8},{4,12},{8,0},{12,4},{1,9},{5,13},{9,1},{13,5},{2,10},{6,14},... | collective-permute-start | bytes 393224 | tf_op jit(solution)/shard_map/ppermute | solution.py:279
  44.3 8.8 %collective-permute-done.18.refs_1_ = f32[2,4,64,128]{3,2,1,0:T(8,128)S(1)} collective-permute-done((f32[2,4,64,128]{3,2,1,0:T(8,128)S(1)}, f32[2,4,64,128]{3,2,1,0:T(8,128)S(1)}, u32[]{:S(2)}, u32[]{:S(2)}) %collective-permute-start.18) | collective-permute-done | bytes 262176 | tf_op jit(solution)/shard_map/ppermute | solution.py:272
  53.1 0.1 collective-permute-start.19
  53.2 0.1 pad_add_fusion.scalars
  53.3 0.0 collective-permute-done.10.refs_5_
  53.3 0.0 collective-permute-done.17.refs_8_
  53.3 1.4 %gathered.1 = f32[2,8,64,128]{3,2,1,0:T(8,128)} custom-call(s32[2]{0:T(128)S(1)} %pad_add_fusion.scalars, f32[2,4,64,128]{3,2,1,0:T(8,128)S(1)} %get-tuple-element.13.refs_0_, f32[2,4,64,128]{3,2,1,0:T(8,128)S(1)} %collective-permute-done.2.refs_1_, f32[1,4,64,128]{3,2,1,0:T(8,128)S(1)} %collective-permute-done.3.refs_9_.refs_2_, ...), custom_call_target="tpu_custom_call" | custom-call | flops 1024 | bytes 1024 | tf_op jit(solution)/shard_map/gathered/pallas_call | solution.py:124
  54.7 6.2 %collective-permute-done.19 = f32[1,4,64,128]{3,2,1,0:T(8,128)S(1)} collective-permute-done((f32[1,4,64,128]{3,2,1,0:T(8,128)S(1)}, f32[1,4,64,128]{3,2,1,0:T(8,128)S(1)}, u32[]{:S(2)}, u32[]{:S(2)}) %collective-permute-start.19) | collective-permute-done | bytes 131104 | tf_op jit(solution)/shard_map/ppermute | solution.py:279
  60.9 0.7 %fusion.1 = f32[2,8,64,128]{3,2,1,0:T(8,128)} fusion(f32[2,8,64,128]{3,2,1,0:T(8,128)} %gathered.1, s32[]{:T(128)S(6)} %select_n.16, f32[1,4,64,128]{3,2,1,0:T(8,128)S(1)} %collective-permute-done.19, f32[2,4,64,128]{3,2,1,0:T(8,128)S(1)} %collective-permute-done.18.refs_1_, f32[2,4,64,128]{3,2,1,0:T(8,128)S(1)} %get-tuple-element.20.refs_0_), kind=kLoop, calls=%fused_computation.2 | loop fusion | flops 65536 | bytes 524292 | tf_op jit(solution)/shard_map/dynamic_update_slice | solution.py:296
  (9 shorter events, 0.1 us)
Async XLA Ops:
  0.0 5.4 %copy-start = (s32[3,2]{0,1:T(2,128)S(1)}, s32[3,2]{0,1:T(2,128)}, u32[]{:S(2)}) copy-start(s32[3,2]{0,1:T(2,128)} %param.7) | copy-start | bytes 76
  0.0 7.1 %collective-permute-start.1 = (f32[2,8,256,128]{3,2,1,0:T(8,128)}, f32[2,8,256,128]{3,2,1,0:T(8,128)}, u32[]{:S(2)}, u32[]{:S(2)}) collective-permute-start(f32[2,8,256,128]{3,2,1,0:T(8,128)} %refs_2_.7), channel_id=1, source_target_pairs={{0,1},{1,0},{2,3},{3,2},{4,5},{5,4},{6,7},{7,6},{8,9},{9,8},{10,11... | collective-permute-start | bytes 6291464 | tf_op jit(solution)/shard_map/ppermute | solution.py:235
  0.5 6.6 %collective-permute-start = (f32[3,2,128,256]{3,2,1,0:T(8,128)}, f32[3,2,128,256]{3,2,1,0:T(8,128)S(1)}, u32[]{:S(2)}, u32[]{:S(2)}) collective-permute-start(f32[3,2,128,256]{3,2,1,0:T(8,128)} %refs_0_.7), channel_id=1, source_target_pairs={{0,1},{1,0},{2,3},{3,2},{4,5},{5,4},{6,7},{7,6},{8,9},{9,8},{10,11... | collective-permute-start | bytes 2359304 | tf_op jit(solution)/shard_map/ppermute | solution.py:236
  2.4 17.2 %collective-permute-start.5 = (f32[4,256,128]{2,1,0:T(8,128)}, f32[4,256,128]{2,1,0:T(8,128)}, u32[]{:S(2)}, u32[]{:S(2)}) collective-permute-start(f32[4,256,128]{2,1,0:T(8,128)} %edge.2.earlier), channel_id=1, source_target_pairs={{0,2},{2,0},{1,3},{3,1},{4,6},{6,4},{5,7},{7,5},{8,10},{10,8},{9,1... | collective-permute-start | bytes 1572872 | tf_op jit(solution)/shard_map/ppermute | solution.py:251
  11.2 8.4 %collective-permute-start.2 = (f32[2,4,64,128]{3,2,1,0:T(8,128)S(1)}, f32[2,4,64,128]{3,2,1,0:T(8,128)S(1)}, u32[]{:S(2)}, u32[]{:S(2)}) collective-permute-start(f32[2,4,64,128]{3,2,1,0:T(8,128)S(1)} %get-tuple-element.14), channel_id=1, source_target_pairs={{0,4},{4,0},{8,12},{12,8},{1,5},{5,1},{9,13},{13,9},{2,6},{6,2},{1... | collective-permute-start | bytes 786440 | tf_op jit(solution)/shard_map/ppermute | solution.py:272
  14.0 18.4 %collective-permute-start.12 = (f32[4,256,128]{2,1,0:T(8,128)S(1)}, f32[4,256,128]{2,1,0:T(8,128)S(1)}, u32[]{:S(2)}, u32[]{:S(2)}) collective-permute-start(f32[4,256,128]{2,1,0:T(8,128)S(1)} %edge.3), channel_id=1, source_target_pairs={{0,2},{2,0},{1,3},{3,1},{4,6},{6,4},{5,7},{7,5},{8,10},{10,8},{9,1... | collective-permute-start | bytes 1572872 | tf_op jit(solution)/shard_map/ppermute | solution.py:251
  20.8 2.2 %collective-permute-start.9 = (f32[1,256,128]{2,1,0:T(8,128)S(1)}, f32[1,256,128]{2,1,0:T(8,128)S(1)}, u32[]{:S(2)}, u32[]{:S(2)}) collective-permute-start(f32[1,256,128]{2,1,0:T(8,128)S(1)} %get-tuple-element.25), channel_id=1, source_target_pairs={{0,1},{1,0},{2,3},{3,2},{4,5},{5,4},{6,7},{7,6},{8,9},{9,8},{10,11... | collective-permute-start | bytes 393224 | tf_op jit(solution)/shard_map/ppermute | solution.py:261
  20.8 11.5 %collective-permute-start.4 = (f32[2,4,64,128]{3,2,1,0:T(8,128)S(1)}, f32[2,4,64,128]{3,2,1,0:T(8,128)S(1)}, u32[]{:S(2)}, u32[]{:S(2)}) collective-permute-start(f32[2,4,64,128]{3,2,1,0:T(8,128)S(1)} %get-tuple-element.15.refs_2_), channel_id=1, source_target_pairs={{0,4},{4,0},{8,12},{12,8},{1,5},{5,1},{9,13},{13,9},{2,6},{6,2},{1... | collective-permute-start | bytes 786440 | tf_op jit(solution)/shard_map/ppermute | solution.py:272
  22.5 1.3 %collective-permute-start.8 = (f32[1,256,128]{2,1,0:T(8,128)S(1)}, f32[1,256,128]{2,1,0:T(8,128)S(1)}, u32[]{:S(2)}, u32[]{:S(2)}) collective-permute-start(f32[1,256,128]{2,1,0:T(8,128)S(1)} %get-tuple-element.26), channel_id=1, source_target_pairs={{0,1},{1,0},{2,3},{3,2},{4,5},{5,4},{6,7},{7,6},{8,9},{9,8},{10,11... | collective-permute-start | bytes 393224 | tf_op jit(solution)/shard_map/ppermute | solution.py:261
  22.6 3.8 %collective-permute-start.7 = (f32[1,256,128]{2,1,0:T(8,128)S(1)}, f32[1,256,128]{2,1,0:T(8,128)S(1)}, u32[]{:S(2)}, u32[]{:S(2)}) collective-permute-start(f32[1,256,128]{2,1,0:T(8,128)S(1)} %get-tuple-element.27), channel_id=1, source_target_pairs={{0,1},{1,0},{2,3},{3,2},{4,5},{5,4},{6,7},{7,6},{8,9},{9,8},{10,11... | collective-permute-start | bytes 393224 | tf_op jit(solution)/shard_map/ppermute | solution.py:261
  23.0 3.4 %collective-permute-start.6 = (f32[1,256,128]{2,1,0:T(8,128)S(1)}, f32[1,256,128]{2,1,0:T(8,128)S(1)}, u32[]{:S(2)}, u32[]{:S(2)}) collective-permute-start(f32[1,256,128]{2,1,0:T(8,128)S(1)} %get-tuple-element.28), channel_id=1, source_target_pairs={{0,1},{1,0},{2,3},{3,2},{4,5},{5,4},{6,7},{7,6},{8,9},{9,8},{10,11... | collective-permute-start | bytes 393224 | tf_op jit(solution)/shard_map/ppermute | solution.py:261
  23.8 9.7 %collective-permute-start.3 = (f32[1,4,64,128]{3,2,1,0:T(8,128)S(1)}, f32[1,4,64,128]{3,2,1,0:T(8,128)S(1)}, u32[]{:S(2)}, u32[]{:S(2)}) collective-permute-start(f32[1,4,64,128]{3,2,1,0:T(8,128)S(1)} %summed.4.refs_1_), channel_id=1, source_target_pairs={{0,8},{4,12},{8,0},{12,4},{1,9},{5,13},{9,1},{13,5},{2,10},{6,14},... | collective-permute-start | bytes 393224 | tf_op jit(solution)/shard_map/ppermute | solution.py:279
  32.5 2.5 %collective-permute-start.16 = (f32[1,256,128]{2,1,0:T(8,128)S(1)}, f32[1,256,128]{2,1,0:T(8,128)S(1)}, u32[]{:S(2)}, u32[]{:S(2)}) collective-permute-start(f32[1,256,128]{2,1,0:T(8,128)S(1)} %get-tuple-element.21), channel_id=1, source_target_pairs={{0,1},{1,0},{2,3},{3,2},{4,5},{5,4},{6,7},{7,6},{8,9},{9,8},{10,11... | collective-permute-start | bytes 393224 | tf_op jit(solution)/shard_map/ppermute | solution.py:261
  32.5 2.4 %collective-permute-start.15 = (f32[1,256,128]{2,1,0:T(8,128)S(1)}, f32[1,256,128]{2,1,0:T(8,128)S(1)}, u32[]{:S(2)}, u32[]{:S(2)}) collective-permute-start(f32[1,256,128]{2,1,0:T(8,128)S(1)} %get-tuple-element.22), channel_id=1, source_target_pairs={{0,1},{1,0},{2,3},{3,2},{4,5},{5,4},{6,7},{7,6},{8,9},{9,8},{10,11... | collective-permute-start | bytes 393224 | tf_op jit(solution)/shard_map/ppermute | solution.py:261
  33.0 1.9 %collective-permute-start.14 = (f32[1,256,128]{2,1,0:T(8,128)S(1)}, f32[1,256,128]{2,1,0:T(8,128)S(1)}, u32[]{:S(2)}, u32[]{:S(2)}) collective-permute-start(f32[1,256,128]{2,1,0:T(8,128)S(1)} %get-tuple-element.23), channel_id=1, source_target_pairs={{0,1},{1,0},{2,3},{3,2},{4,5},{5,4},{6,7},{7,6},{8,9},{9,8},{10,11... | collective-permute-start | bytes 393224 | tf_op jit(solution)/shard_map/ppermute | solution.py:261
  33.1 1.9 %collective-permute-start.13 = (f32[1,256,128]{2,1,0:T(8,128)S(1)}, f32[1,256,128]{2,1,0:T(8,128)S(1)}, u32[]{:S(2)}, u32[]{:S(2)}) collective-permute-start(f32[1,256,128]{2,1,0:T(8,128)S(1)} %get-tuple-element.24), channel_id=1, source_target_pairs={{0,1},{1,0},{2,3},{3,2},{4,5},{5,4},{6,7},{7,6},{8,9},{9,8},{10,11... | collective-permute-start | bytes 393224 | tf_op jit(solution)/shard_map/ppermute | solution.py:261
  33.6 9.6 %collective-permute-start.11 = (f32[2,4,64,128]{3,2,1,0:T(8,128)S(1)}, f32[2,4,64,128]{3,2,1,0:T(8,128)S(1)}, u32[]{:S(2)}, u32[]{:S(2)}) collective-permute-start(f32[2,4,64,128]{3,2,1,0:T(8,128)S(1)} %get-tuple-element.17.refs_2_), channel_id=1, source_target_pairs={{0,4},{4,0},{8,12},{12,8},{1,5},{5,1},{9,13},{13,9},{2,6},{6,2},{1... | collective-permute-start | bytes 786440 | tf_op jit(solution)/shard_map/ppermute | solution.py:272
  39.3 13.8 %collective-permute-start.18 = (f32[2,4,64,128]{3,2,1,0:T(8,128)S(1)}, f32[2,4,64,128]{3,2,1,0:T(8,128)S(1)}, u32[]{:S(2)}, u32[]{:S(2)}) collective-permute-start(f32[2,4,64,128]{3,2,1,0:T(8,128)S(1)} %get-tuple-element.19.refs_2_), channel_id=1, source_target_pairs={{0,4},{4,0},{8,12},{12,8},{1,5},{5,1},{9,13},{13,9},{2,6},{6,2},{1... | collective-permute-start | bytes 786440 | tf_op jit(solution)/shard_map/ppermute | solution.py:272
  40.0 13.3 %collective-permute-start.10 = (f32[1,4,64,128]{3,2,1,0:T(8,128)S(1)}, f32[1,4,64,128]{3,2,1,0:T(8,128)S(1)}, u32[]{:S(2)}, u32[]{:S(2)}) collective-permute-start(f32[1,4,64,128]{3,2,1,0:T(8,128)S(1)} %summed.5.refs_1_), channel_id=1, source_target_pairs={{0,8},{4,12},{8,0},{12,4},{1,9},{5,13},{9,1},{13,5},{2,10},{6,14},... | collective-permute-start | bytes 393224 | tf_op jit(solution)/shard_map/ppermute | solution.py:279
  43.1 10.2 %collective-permute-start.17 = (f32[1,4,64,128]{3,2,1,0:T(8,128)S(1)}, f32[1,4,64,128]{3,2,1,0:T(8,128)S(1)}, u32[]{:S(2)}, u32[]{:S(2)}) collective-permute-start(f32[1,4,64,128]{3,2,1,0:T(8,128)S(1)} %summed.6), channel_id=1, source_target_pairs={{0,8},{4,12},{8,0},{12,4},{1,9},{5,13},{9,1},{13,5},{2,10},{6,14},... | collective-permute-start | bytes 393224 | tf_op jit(solution)/shard_map/ppermute | solution.py:279
  53.1 7.8 %collective-permute-start.19 = (f32[1,4,64,128]{3,2,1,0:T(8,128)S(1)}, f32[1,4,64,128]{3,2,1,0:T(8,128)S(1)}, u32[]{:S(2)}, u32[]{:S(2)}) collective-permute-start(f32[1,4,64,128]{3,2,1,0:T(8,128)S(1)} %summed.7), channel_id=1, source_target_pairs={{0,8},{4,12},{8,0},{12,4},{1,9},{5,13},{9,1},{13,5},{2,10},{6,14},... | collective-permute-start | bytes 393224 | tf_op jit(solution)/shard_map/ppermute | solution.py:279
